TPU v7x, 128 devices: a whole 4x4x4 slice. The times are simulated.
128 devices in a mesh: row: 2 (over core), col: 4 (over x), depth: 16 (over z, y).
Axes of the slice: x: 4, y: 4, z: 4, core: 2. Of those that a mesh axis runs over, the one named last changes fastest.
Arguments:
- tokens: bfloat16 [3072, 4096], P(('col', 'depth'), 'row'), may hold values from -6 to 6
- gate_weight: bfloat16 [4096, 14336], P('row', 'col'), may hold values from -0.09375 to 0.09375
- up_weight: bfloat16 [4096, 14336], P('row', 'col'), may hold values from -0.09375 to 0.09375
- down_weight: bfloat16 [14336, 4096], P('col', 'row'), may hold values from -0.046875 to 0.046875
- cotangent: bfloat16 [3072, 4096], P(('col', 'depth'), 'row'), may hold values from -16 to 16
Outputs:
- mixed: bfloat16 [3072, 4096], P(('col', 'depth'), 'row')
- input_grad: bfloat16 [3072, 4096], P(('col', 'depth'), 'row')
- gate_grad: bfloat16 [4096, 14336], P('row', ('col', 'depth'))
- up_grad: bfloat16 [4096, 14336], P('row', ('col', 'depth'))
- down_grad: bfloat16 [14336, 4096], P('col', ('row', 'depth'))
All inputs are finite; a program needn't handle non-finite values.
Results may differ from a plain program's by a relative error of at most 0.027.
Values may be sent and summed in bfloat16 or wider, within the bound.
No kernel may reach another device: no remote copies, remote signals or barrier semaphores. Data moves between devices by JAX's collectives and lax.ppermute only.
A program may use at most 192 MiB of HBM per device.

v0:
```python
import functools

import jax
import jax.numpy as jnp
from jax import lax
from jax.experimental import pallas as pl
from jax.experimental.pallas import tpu as pltpu
from jax.sharding import PartitionSpec as P

N_COL = 4
N_DEPTH = 16
SIDE = 4
PIECE = 256
BF16 = jnp.bfloat16
F32 = jnp.float32
LAST = (((1,), (1,)), ((), ()))
MIB = 1024 * 1024


def shifted(axis, index, step):
    if axis == "x":
        return (index + step) % N_COL
    z, y = divmod(index, SIDE)
    if axis == "y":
        return z * SIDE + (y + step) % SIDE
    return ((z + step) % SIDE) * SIDE + y


def extent(axis):
    return N_COL if axis == "x" else N_DEPTH


def mesh_axis(axis):
    return "col" if axis == "x" else "depth"


def hop(array, axis):
    n = extent(axis)
    pairs = [
        (core * n + i, core * n + shifted(axis, i, 1 - 2 * core))
        for core in range(2)
        for i in range(n)
    ]
    return lax.ppermute(array, ("row", mesh_axis(axis)), pairs)


def shift(array, axis, step):
    pairs = [(i, shifted(axis, i, step)) for i in range(extent(axis))]
    return lax.ppermute(array, mesh_axis(axis), pairs)


def swap(array):
    return lax.ppermute(array, "row", [(0, 1), (1, 0)])


def ring(array, axis):
    pieces = [array]
    for _ in range(SIDE - 1):
        pieces.append(hop(pieces[-1], axis))
    return pieces


def tie(values, *deps):
    return lax.optimization_barrier((*values, *deps))[: len(values)]


def regroup_kernel(n_in, plans, core_ref, *refs):
    def copy(plan):
        for out_ref, rows in zip(refs[n_in:], plan):
            at = 0
            for source, start, count in rows:
                out_ref[at : at + count] = refs[source][start : start + count]
                at += count

    if len(plans) == 1:
        copy(plans[0])
    else:
        for c, plan in enumerate(plans):
            pl.when(core_ref[0] == c)(functools.partial(copy, plan))


def regroup(core, arrays, *plans):
    features = arrays[0].shape[1]
    counts = [sum(count for _, _, count in rows) for rows in plans[0]]
    return pl.pallas_call(
        lambda *refs: regroup_kernel(len(arrays), plans, *refs),
        in_specs=[pl.BlockSpec(memory_space=pltpu.SMEM)]
        + [pl.BlockSpec(memory_space=pltpu.VMEM)] * len(arrays),
        out_shape=[jax.ShapeDtypeStruct((n, features), BF16) for n in counts],
        cost_estimate=cost(1),
        compiler_params=pltpu.CompilerParams(vmem_limit_bytes=16 * MIB),
    )(core, *arrays)


def times_transpose(left, right):
    return lax.dot_general(left, right, LAST, preferred_element_type=F32)


def plain(left, right):
    return jnp.dot(left, right, preferred_element_type=F32)


def gate_up_grads(gate, up, hidden_grad):
    s = jax.nn.sigmoid(gate)
    grad_up = (hidden_grad * gate * s).astype(BF16)
    grad_gate = (hidden_grad * up * s * (1.0 + gate * (1.0 - s))).astype(BF16)
    return grad_gate, grad_up


def cost(megabytes):
    return pl.CostEstimate(flops=0, bytes_accessed=int(megabytes * 1e6), transcendentals=0)


def own_partials_kernel(n_parts, sides, *refs):
    weights, out_ref = refs[len(sides) * n_parts : -1], refs[-1]
    rows = out_ref.shape[1]
    at = 0
    for s, (side, weight_ref) in enumerate(zip(sides, weights)):
        left = jnp.concatenate([x[...] for x in refs[s * n_parts : (s + 1) * n_parts]], axis=0)
        product = (times_transpose if side else plain)(left, weight_ref[...]).astype(BF16)
        width = product.shape[1]
        for p in range(n_parts):
            out_ref[p, :, at : at + width] = product[p * rows : (p + 1) * rows]
        at += width


def own_partials(pieces, weights, sides, steps=2):
    n_parts = len(pieces[0])
    flat = [x for side in pieces for x in side]
    rows, features = PIECE, flat[0][0].shape[1]
    used = [weights[side] for side in sides]
    widths = [w.shape[0] if side else w.shape[1] for side, w in zip(sides, used)]

    def spec(at):
        return pl.BlockSpec((rows // steps, features), lambda i: (at * steps + i, 0))

    return pl.pallas_call(
        lambda *refs: own_partials_kernel(n_parts, sides, *refs),
        grid=(steps,),
        in_specs=[spec(at) for _, at in flat]
        + [pl.BlockSpec(w.shape, lambda i: (0, 0)) for w in used],
        out_specs=pl.BlockSpec((n_parts, rows // steps, sum(widths)), lambda i: (0, i, 0)),
        out_shape=jax.ShapeDtypeStruct((n_parts, rows, sum(widths)), BF16),
        cost_estimate=cost(1),
        compiler_params=pltpu.CompilerParams(vmem_limit_bytes=32 * MIB),
    )(*[x for x, _ in flat], *used)


def row_sum(mine_ref, theirs_ref):
    n = mine_ref.shape[1] // SIDE
    theirs = jnp.concatenate(
        [theirs_ref[0, (-k % SIDE) * n : (-k % SIDE + 1) * n] for k in range(SIDE)], axis=0
    )
    return mine_ref[0].astype(F32) + theirs.astype(F32)


def hidden_kernel(mine_ref, theirs_ref, out_ref):
    wide = out_ref.shape[0]
    total = row_sum(mine_ref, theirs_ref)
    gate, up = total[:, :wide], total[:, wide:]
    out_ref[...] = (gate * jax.nn.sigmoid(gate) * up).T.astype(BF16)


def grads_kernel(mine_ref, theirs_ref, mine_grad_ref, theirs_grad_ref, out_ref):
    wide = out_ref.shape[0] // 2
    total = row_sum(mine_ref, theirs_ref)
    gate, up = total[:, :wide], total[:, wide:]
    hidden_grad = row_sum(mine_grad_ref, theirs_grad_ref)
    s = jax.nn.sigmoid(gate)
    out_ref[:wide] = (hidden_grad * up * s * (1.0 + gate * (1.0 - s))).T.astype(BF16)
    out_ref[wide:] = (hidden_grad * gate * s).T.astype(BF16)


def activations(kernel, width, *args):
    n_parts, rows, _ = args[0][0].shape

    def spec(columns, block):
        return pl.BlockSpec((1, rows, columns), lambda i: (i, 0, block))

    return pl.pallas_call(
        kernel,
        grid=(n_parts,),
        in_specs=[spec(columns, block) for _, columns, block in args],
        out_specs=pl.BlockSpec((width, rows), lambda i: (0, i)),
        out_shape=jax.ShapeDtypeStruct((width, n_parts * rows), BF16),
        cost_estimate=cost(1),
        compiler_params=pltpu.CompilerParams(vmem_limit_bytes=32 * MIB),
    )(*[x for x, _, _ in args])


def weight_grad_kernel(n_groups, n_parts, before, own, kind, *refs):
    left = refs[:n_groups]
    right = refs[n_groups : n_groups + n_groups * n_parts]
    outs = refs[n_groups + n_groups * n_parts :]
    rows = right[0].shape[0]
    total = None
    if before:
        total, outs = outs[0][...], outs[1:]
    for k in range(n_groups):
        for p in range(n_parts):
            term = plain(left[k][:, p * rows : (p + 1) * rows], right[k * n_parts + p][...])
            total = term if total is None else total + term
    if kind == "sum":
        outs[0][...] = total
    elif kind == "blocks":
        width = outs[0].shape[2]
        for k in range(outs[0].shape[0]):
            outs[0][k] = total[:own, k * width : (k + 1) * width].astype(BF16)
    else:
        half = total.shape[0] // 2
        outs[0][...] = total[:own].astype(BF16)
        outs[1][...] = total[half : half + own].astype(BF16)


def weight_grad(left, right, kind, own, before=None, block=512):
    n_groups, n_parts = len(left), len(right[0])
    flat = [piece for group in right for piece in group]
    rows, features = PIECE, flat[0][0].shape[1]
    hidden = left[0].shape[0]

    def spec(at):
        return pl.BlockSpec((rows, block), lambda i: (at, i))

    in_specs = [pl.BlockSpec(x.shape, lambda i: (0, 0)) for x in left]
    in_specs += [spec(at) for _, at in flat]
    args = [*left, *[x for x, _ in flat]]
    if before is not None:
        in_specs.append(pl.BlockSpec((hidden, block), lambda i: (0, i)))
        args.append(before)
    if kind == "sum":
        out_shape = [jax.ShapeDtypeStruct((hidden, features), F32)]
        out_specs = [pl.BlockSpec((hidden, block), lambda i: (0, i))]
    elif kind == "blocks":
        width = features // N_DEPTH
        out_shape = [jax.ShapeDtypeStruct((N_DEPTH, own, width), BF16)]
        out_specs = [pl.BlockSpec((block // width, own, width), lambda i: (i, 0, 0))]
    else:
        out_shape = [jax.ShapeDtypeStruct((own, features), BF16)] * 2
        out_specs = [pl.BlockSpec((own, block), lambda i: (0, i))] * 2
    return pl.pallas_call(
        lambda *refs: weight_grad_kernel(n_groups, n_parts, before is not None, own, kind, *refs),
        grid=(features // block,),
        in_specs=in_specs,
        out_specs=out_specs,
        out_shape=out_shape,
        cost_estimate=cost(1),
        compiler_params=pltpu.CompilerParams(vmem_limit_bytes=40 * MIB),
    )(*args)


def sums_at(refs, columns):
    return [
        mine[:, columns].astype(F32) + theirs[:, columns].astype(F32)
        for mine, theirs in zip(refs[::2], refs[1::2])
    ]


def mixed_kernel(*refs):
    weight_ref, out_ref, hidden_ref = refs[4:]

    @pl.when(pl.program_id(0) == 0)
    def _():
        for at in range(0, hidden_ref.shape[1], 512):
            columns = slice(at, at + 512)
            gate, up = sums_at(refs[:4], columns)
            hidden_ref[:, columns] = (gate * jax.nn.sigmoid(gate) * up).astype(BF16)

    out_ref[...] = plain(hidden_ref[...], weight_ref[...]).astype(BF16)


def whole(array):
    return pl.BlockSpec(array.shape, lambda i: (0, 0))


def mixed_product(gate_up, weight, block=512):
    width, features = weight.shape
    tokens = gate_up[0].shape[0]
    return pl.pallas_call(
        mixed_kernel,
        grid=(features // block,),
        in_specs=[*map(whole, gate_up), pl.BlockSpec((width, block), lambda i: (0, i))],
        out_specs=pl.BlockSpec((tokens, block), lambda i: (0, i)),
        out_shape=jax.ShapeDtypeStruct((tokens, features), BF16),
        scratch_shapes=[pltpu.VMEM((tokens, width), BF16)],
        cost_estimate=cost(1),
        compiler_params=pltpu.CompilerParams(vmem_limit_bytes=52 * MIB),
    )(*gate_up, weight)


def slice_grads_kernel(*refs):
    refs[6][...], refs[7][...] = gate_up_grads(*sums_at(refs[:6], slice(None)))


def slice_grads(values, block=512):
    tokens, width = values[0].shape
    spec = pl.BlockSpec((tokens, block), lambda i: (0, i))
    return pl.pallas_call(
        slice_grads_kernel,
        grid=(width // block,),
        in_specs=[spec] * 6,
        out_specs=[spec] * 2,
        out_shape=[jax.ShapeDtypeStruct((tokens, width), BF16)] * 2,
        cost_estimate=cost(1),
        compiler_params=pltpu.CompilerParams(vmem_limit_bytes=32 * MIB),
    )(*values)


def input_kernel(grad_gate_ref, grad_up_ref, gate_ref, up_ref, out_ref):
    total = times_transpose(grad_gate_ref[...], gate_ref[...])
    total += times_transpose(grad_up_ref[...], up_ref[...])
    out_ref[...] = total.astype(BF16)


def input_product(grads, gate_weight, up_weight, block=256):
    features, width = gate_weight.shape
    tokens = grads[0].shape[0]
    rows = pl.BlockSpec((block, width), lambda i: (i, 0))
    return pl.pallas_call(
        input_kernel,
        grid=(features // block,),
        in_specs=[*map(whole, grads), rows, rows],
        out_specs=pl.BlockSpec((tokens, block), lambda i: (0, i)),
        out_shape=jax.ShapeDtypeStruct((tokens, features), BF16),
        cost_estimate=cost(1),
        compiler_params=pltpu.CompilerParams(vmem_limit_bytes=52 * MIB),
    )(*grads, gate_weight, up_weight)


def added(terms, start, count):
    total = terms[0][start : start + count].astype(F32)
    for term in terms[1:]:
        total = total + term[start : start + count].astype(F32)
    return total.astype(BF16)


def per_device(tokens, gate_weight, up_weight, down_weight, cotangent):
    core = lax.axis_index("row").astype(jnp.int32).reshape(1)
    depth = lax.axis_index("depth")
    rows = tokens.shape[0]
    hidden_width = gate_weight.shape[1]
    own = hidden_width // N_DEPTH
    wide = -(-own // 128) * 128

    n = rows // 3
    thirds = [[(0, p * n, n), (1, p * n, n)] for p in range(3)]
    mine, zs, ys = regroup(
        core, [tokens, cotangent], [thirds[0] + thirds[1] + thirds[2], thirds[1], thirds[2]]
    )
    xs = [mine] + [shift(mine, "x", s) for s in (1, 2, -1)]
    zs, ys = ring(zs, "z"), ring(ys, "y")

    def joined(pieces, half):
        orders = ((0, 1, 2, 3), (0, 3, 2, 1))
        plans = [[[(i, c * half, half) for c in range(2) for i in order]] for order in orders]
        return regroup(core, pieces, *plans)[0]

    def stacked(pieces, half):
        return regroup(core, pieces, [[(i, c * half, half) for c in range(2) for i in range(4)]])[0]

    panel_plan = [[(i, 2 * n * p + n * c, n) for i in range(4) for p in range(3)] for c in range(2)]
    first_plan = [(i, n * c, n) for c in range(2) for i in range(4)]
    panel, grad_panel, r0 = regroup(core, xs, [*panel_plan, first_plan])
    t0, q0 = joined(zs, n), joined(ys, n)
    r1, t1, q1 = hop(r0, "y"), hop(t0, "x"), hop(q0, "z")

    def own_columns(weight):
        cut = lax.dynamic_slice_in_dim(weight, depth * own, own, axis=1)
        return jnp.pad(cut, ((0, 0), (0, wide - own)))

    own_gate_up = jnp.concatenate([own_columns(gate_weight), own_columns(up_weight)], axis=1)
    own_down = jnp.pad(
        lax.dynamic_slice_in_dim(down_weight, depth * own, own, axis=0), ((0, wide - own), (0, 0))
    )

    (panel_,) = tie((panel,), r0, own_gate_up, own_down)
    gate_part = plain(panel_, gate_weight).astype(BF16)

    (panel_,) = tie((panel,), gate_part, r1, t1, q1)
    (r1_, t1_, q1_) = tie((r1, t1, q1), gate_part)
    r2, t2, q2 = hop(r1_, "y"), hop(t1_, "x"), hop(q1_, "z")
    up_part = plain(panel_, up_weight).astype(BF16)
    gate_theirs = swap(gate_part)

    (grad_panel,) = tie((grad_panel,), up_part, r2, t2, q2, gate_theirs)
    (r2_, t2_, q2_) = tie((r2, t2, q2), up_part)
    r3, t3, q3 = hop(r2_, "y"), hop(t2_, "x"), hop(q2_, "z")
    up_theirs = swap(up_part)
    grad_part = times_transpose(grad_panel, down_weight).astype(BF16)

    r0, r1, r2, r3 = tie((r0, r1, r2, r3), grad_part, up_theirs)
    t0, t1, t2, t3 = tie((t0, t1, t2, t3), grad_part)
    q0, q1, q2, q3 = tie((q0, q1, q2, q3), grad_part)
    grad_theirs = swap(grad_part)
    axes = ("z", "y", "x")

    def hops(pieces, *deps):
        return [hop(*tie((x,), *deps), axis) for x, axis in zip(pieces, axes)]

    both = [[stacked(x, 4 * n) for x in ((r0, r1, r2, r3), (t0, t1, t2, t3), (q0, q1, q2, q3))]]
    both.append(hops(both[0]))
    toks, cots = [[(x, 0) for x in both[0]]], [[(x, 1) for x in both[0]]]
    (gate_part_,) = tie((gate_part,), *both[0])
    gate_up = (gate_theirs, up_part, up_theirs)
    mixed_part = mixed_product((gate_part_, *gate_up), down_weight)
    (own_down_,) = tie((own_down,), mixed_part)
    u0 = own_partials([toks[0], cots[0]], (own_gate_up, own_down_), (0, 1))
    v0 = swap(u0)
    (gate_part_,) = tie((gate_part,), u0)
    grads = slice_grads((gate_part_, *gate_up, grad_part, grad_theirs))

    both.append(hops(both[1], *grads))
    toks.append([(x, 0) for x in both[1]])
    cots.append([(x, 1) for x in both[1]])
    input_part = input_product(tie(tuple(grads), *both[1]), gate_weight, up_weight)
    (own_down_,) = tie((own_down,), input_part)
    u1 = own_partials([toks[1], cots[1]], (own_gate_up, own_down_), (0, 1))
    v1 = swap(u1)
    back_plan = [[(p, back * rows, rows) for p in range(2)] for back in range(N_COL)]
    sums = regroup(core, [mixed_part, input_part], back_plan)

    both.append(hops(both[2], u1, v0, v1, *sums))
    toks.append([(x, 0) for x in both[2]])
    cots.append([(x, 1) for x in both[2]])
    (own_down_,) = tie((own_down,), u1, *both[2])
    u2 = own_partials([toks[2], cots[2]], (own_gate_up, own_down_), (0, 1))
    v2 = swap(u2)

    def hidden_of(mine, theirs):
        return activations(hidden_kernel, wide, *[(x, 2 * wide, 0) for x in (mine, theirs)])

    def grads_of(mine, theirs, *grads):
        pre = [(x, 2 * wide, 0) for x in (mine, theirs)]
        return activations(grads_kernel, 2 * wide, *pre, *[(x, wide, at) for x, at in grads])

    (u0,) = tie((u0,), u2)
    h0 = hidden_of(u0, v0)
    d0 = grads_of(u0, v0, (u0, 2), (v0, 2))
    (u2,) = tie((u2,), d0)
    h2 = hidden_of(u2, v2)
    d2 = grads_of(u2, v2, (u2, 2), (v2, 2))
    (h2,) = tie((h2,), d2)
    (down_early,) = weight_grad([h0, h2], [cots[0], cots[2]], "sum", own)
    (d2,) = tie((d2,), down_early)
    (grads_early,) = weight_grad([d0, d2], [toks[0], toks[2]], "sum", own)

    toks.append([(x, 0) for x in both[3]])
    cots.append([(x, 1) for x in both[3]])
    (own_gate_up_,) = tie((own_gate_up,), grads_early, *both[3])
    u3 = own_partials([toks[3]], (own_gate_up_, None), (0,))
    v3 = swap(u3)
    h3 = hidden_of(u3, v1)
    (u1,) = tie((u1,), h3)
    h1 = hidden_of(u1, v3)
    (down_blocks,) = weight_grad([h1, h3], [cots[1], cots[3]], "blocks", own, before=down_early)
    down_grad = lax.all_to_all(down_blocks, "depth", split_axis=0, concat_axis=0, tiled=True)

    (own_down_,) = tie((own_down,), h3)
    w3 = own_partials([cots[3]], (None, own_down_), (1,))
    z3 = swap(w3)
    (u3,) = tie((u3,), down_blocks)
    d3 = grads_of(u3, v1, (w3, 0), (v1, 2))
    sums = tie(tuple(sums), u3)
    sums = [sums[0]] + [shift(sums[back], "x", -back) for back in range(1, N_COL)]
    d1 = grads_of(u1, v3, (u1, 2), (z3, 0))
    gate_grad, up_grad = weight_grad(
        [d1, d3], [toks[1], toks[3]], "pair", own, before=grads_early
    )
    down_grad = down_grad.reshape(hidden_width, -1)
    sums = tie(tuple(sums), gate_grad)
    mixed, input_grad = added(sums, 0, rows), added(sums, rows, rows)
    return mixed, input_grad, gate_grad.T, up_grad.T, down_grad


def solution(mesh):
    placed = (
        P(("col", "depth"), "row"),
        P("row", "col"),
        P("row", "col"),
        P("col", "row"),
        P(("col", "depth"), "row"),
    )
    return jax.shard_map(
        per_device,
        mesh=mesh,
        in_specs=placed,
        out_specs=(
            P(("col", "depth"), "row"),
            P(("col", "depth"), "row"),
            P("row", ("col", "depth")),
            P("row", ("col", "depth")),
            P("col", ("row", "depth")),
        ),
        check_vma=False,
    )
```

profile of v0, /device:TPU:1, one launch (start us, length us, event | category | flops | bytes accessed | tf_op | source)
XLA Modules:
  0.0 201.1 jit_solution(6830500449581347373)
XLA Ops:
  4.6 2.5 %collective-permute-start.1 = (bf16[96,2048]{1,0:T(8,128)(2,1)S(1)}, bf16[96,2048]{1,0:T(8,128)(2,1)S(1)}, u32[]{:S(2)}, u32[]{:S(2)}) collective-permute-start(bf16[96,2048]{1,0:T(8,128)(2,1)S(1)} %get-tuple-element.69.refs_1_), channel_id=1, source_target_pairs={{0,32},{16,48},{32,0},{48,16},{1,33},{17,49},{33,1},{49,17},{2,34}... | collective-permute-start | bytes 1179656 | tf_op jit(solution)/shard_map/ppermute | solution.py:49
  8.3 2.7 %collective-permute-start.8 = (bf16[32,2048]{1,0:T(8,128)(2,1)S(1)}, bf16[32,2048]{1,0:T(8,128)(2,1)S(1)}, u32[]{:S(2)}, u32[]{:S(2)}) collective-permute-start(bf16[32,2048]{1,0:T(8,128)(2,1)S(1)} %get-tuple-element.74.refs_1_), channel_id=1, source_target_pairs={{0,1},{1,2},{2,3},{3,0},{4,5},{5,6},{6,7},{7,4},{8,9},{9,10},{10,1... | collective-permute-start | bytes 393224 | tf_op jit(solution)/shard_map/ppermute | solution.py:44
  11.0 3.8 %collective-permute-start.4 = (bf16[32,2048]{1,0:T(8,128)(2,1)S(1)}, bf16[32,2048]{1,0:T(8,128)(2,1)S(1)}, u32[]{:S(2)}, u32[]{:S(2)}) collective-permute-start(bf16[32,2048]{1,0:T(8,128)(2,1)S(1)} %get-tuple-element.73.refs_1_), channel_id=1, source_target_pairs={{0,4},{1,5},{2,6},{3,7},{4,8},{5,9},{6,10},{7,11},{8,12},{9,13},{1... | collective-permute-start | bytes 393224 | tf_op jit(solution)/shard_map/ppermute | solution.py:44
  14.7 3.1 %constant_dynamic-slice_fusion.1 = (bf16[2048,224]{1,0:T(8,128)(2,1)S(1)}, bf16[2048,224]{1,0:T(8,128)(2,1)S(1)}) fusion(bf16[2048,3584]{1,0:T(8,128)(2,1)} %up_ref.1, s32[]{:T(128)S(6)} %select_n.2, bf16[2048,3584]{1,0:T(8,128)(2,1)} %gate_ref.1), kind=kLoop, calls=%fused_computation.11 | loop fusion | bytes 3670020 | tf_op jit(solution)/shard_map/dynamic_slice | solution.py:367
  28.4 2.8 %collective-permute-start.3 = (bf16[128,2048]{1,0:T(8,128)(2,1)S(1)}, bf16[128,2048]{1,0:T(8,128)(2,1)S(1)}, u32[]{:S(2)}, u32[]{:S(2)}) collective-permute-start(bf16[128,2048]{1,0:T(8,128)(2,1)S(1)} %get-tuple-element.82.refs_1_), channel_id=1, source_target_pairs={{0,1},{1,2},{2,3},{3,0},{4,5},{5,6},{6,7},{7,4},{8,9},{9,10},{10,1... | collective-permute-start | bytes 1572872 | tf_op jit(solution)/shard_map/ppermute | solution.py:44
  31.2 3.0 %convolution_convert_fusion.2.refs_0_ = bf16[192,3584]{1,0:T(8,128)(2,1)S(1)} fusion(bf16[192,2048]{1,0:T(8,128)(2,1)S(1)} %get-tuple-element.78, bf16[2048,3584]{1,0:T(8,128)(2,1)S(1)} %copy-done.45), kind=kOutput, calls=%fused_computation.2 | convolution fusion | flops 2819260416 | bytes 16842752 | tf_op jit(solution)/shard_map/dot_general | solution.py:100
  37.4 3.5 %collective-permute-start.12 = (bf16[128,2048]{1,0:T(8,128)(2,1)S(1)}, bf16[128,2048]{1,0:T(8,128)(2,1)}, u32[]{:S(2)}, u32[]{:S(2)}) collective-permute-start(bf16[128,2048]{1,0:T(8,128)(2,1)S(1)} %collective-permute-done.3.refs_2_), channel_id=1, source_target_pairs={{0,1},{1,2},{2,3},{3,0},{4,5},{5,6},{6,7},{7,4},{8,9},{9,10},{10,1... | collective-permute-start | bytes 1572872 | tf_op jit(solution)/shard_map/ppermute | solution.py:44
  40.9 2.3 %collective-permute-start.14 = (bf16[128,2048]{1,0:T(8,128)(2,1)S(1)}, bf16[128,2048]{1,0:T(8,128)(2,1)S(1)}, u32[]{:S(2)}, u32[]{:S(2)}) collective-permute-start(bf16[128,2048]{1,0:T(8,128)(2,1)S(1)} %collective-permute-done.11.refs_2_), channel_id=1, source_target_pairs={{0,4},{1,5},{2,6},{3,7},{4,8},{5,9},{6,10},{7,11},{8,12},{9,13},{1... | collective-permute-start | bytes 1572872 | tf_op jit(solution)/shard_map/ppermute | solution.py:44
  43.1 8.2 %convolution_convert_fusion.1.refs_2_ = bf16[192,3584]{1,0:T(8,128)(2,1)S(1)} fusion(bf16[192,2048]{1,0:T(8,128)(2,1)S(1)} %get-tuple-element.78, bf16[2048,3584]{1,0:T(8,128)(2,1)} %up_ref.1), kind=kOutput, calls=%fused_computation.1 | convolution fusion | flops 2819260416 | bytes 16842752 | tf_op jit(solution)/shard_map/dot_general | solution.py:100
  54.3 3.0 %collective-permute-start.18 = (bf16[128,2048]{1,0:T(8,128)(2,1)S(1)}, bf16[128,2048]{1,0:T(8,128)(2,1)S(1)}, u32[]{:S(2)}, u32[]{:S(2)}) collective-permute-start(bf16[128,2048]{1,0:T(8,128)(2,1)S(1)} %collective-permute-done.13.refs_3_), channel_id=1, source_target_pairs={{0,16},{16,32},{32,48},{48,0},{64,112},{80,64},{96,80},{112,96},{1... | collective-permute-start | bytes 1572872 | tf_op jit(solution)/shard_map/ppermute | solution.py:44
  58.1 2.4 %collective-permute-start.15 = (bf16[128,2048]{1,0:T(8,128)(2,1)}, bf16[128,2048]{1,0:T(8,128)(2,1)}, u32[]{:S(2)}, u32[]{:S(2)}) collective-permute-start(bf16[128,2048]{1,0:T(8,128)(2,1)} %collective-permute-done.12.refs_3_), channel_id=1, source_target_pairs={{0,1},{1,2},{2,3},{3,0},{4,5},{5,6},{6,7},{7,4},{8,9},{9,10},{10,1... | collective-permute-start | bytes 1572872 | tf_op jit(solution)/shard_map/ppermute | solution.py:44
  61.6 11.2 %convolution_convert_fusion.refs_4_ = bf16[192,3584]{1,0:T(8,128)(2,1)} fusion(bf16[192,2048]{1,0:T(8,128)(2,1)S(1)} %get-tuple-element.81, bf16[3584,2048]{1,0:T(8,128)(2,1)} %refs_4_.1), kind=kOutput, calls=%fused_computation | convolution fusion | flops 2819260416 | bytes 16842752 | tf_op jit(solution)/shard_map/dot_general | solution.py:96
  77.9 9.9 %shard_map.99.refs_1_ = bf16[192,2048]{1,0:T(8,128)(2,1)S(1)} custom-call(bf16[192,3584]{1,0:T(8,128)(2,1)} %copy-done.18, bf16[192,3584]{1,0:T(8,128)(2,1)} %copy-done.20, bf16[192,3584]{1,0:T(8,128)(2,1)} %copy-done.22, bf16[192,3584]{1,0:T(8,128)(2,1)} %collective-permute-done.17.refs_3_, bf16[3584,2048]{1,0:T(8,128)(2,1)} %refs_4_.1), custom_call_target="tpu_custom_call" | custom-call | bytes 1000000 | tf_op jit(solution)/shard_map/pallas_call | solution.py:278
  89.1 3.6 %shard_map.100.mine_ref.mine_grad_ref = bf16[3,256,768]{2,1,0:T(8,128)(2,1)} custom-call(bf16[512,2048]{1,0:T(8,128)(2,1)S(1)} %shard_map.96.refs_0_.refs_3_.refs_2_, bf16[512,2048]{1,0:T(8,128)(2,1)S(1)} %shard_map.97.refs_1_.refs_4_.refs_3_, bf16[512,2048]{1,0:T(8,128)(2,1)S(1)} %shard_map.98.refs_2_.refs_5_.refs_4_, ...), custom_call_target="tpu_custom_call" | custom-call | bytes 1000000 | tf_op jit(solution)/shard_map/pallas_call | solution.py:137
  92.7 5.9 %shard_map.101 = (bf16[192,3584]{1,0:T(8,128)(2,1)S(1)}, bf16[192,3584]{1,0:T(8,128)(2,1)S(1)}) custom-call(bf16[192,3584]{1,0:T(8,128)(2,1)S(1)} %copy-done.19, bf16[192,3584]{1,0:T(8,128)(2,1)S(1)} %copy-done.21, bf16[192,3584]{1,0:T(8,128)(2,1)S(1)} %copy-done.23, bf16[192,3584]{1,0:T(8,128)(2,1)} %collective-permute-done.17.refs_3_, ...), custom_call_target="tpu_custom_call" | custom-call | bytes 1000000 | tf_op jit(solution)/shard_map/pallas_call | solution.py:297
  105.4 16.2 %shard_map.102.refs_2_ = bf16[192,2048]{1,0:T(8,128)(2,1)S(1)} custom-call(bf16[192,3584]{1,0:T(8,128)(2,1)} %copy-done.29, bf16[192,3584]{1,0:T(8,128)(2,1)} %copy-done.30, bf16[2048,3584]{1,0:T(8,128)(2,1)} %gate_ref.1, bf16[2048,3584]{1,0:T(8,128)(2,1)} %up_ref.1), custom_call_target="tpu_custom_call" | custom-call | bytes 1000000 | tf_op jit(solution)/shard_map/pallas_call | solution.py:318
  122.8 4.4 %shard_map.104.mine_ref.mine_grad_ref = bf16[3,256,768]{2,1,0:T(8,128)(2,1)S(1)} custom-call(bf16[512,2048]{1,0:T(8,128)(2,1)} %collective-permute-done.21.refs_0_.refs_3_.refs_2_, bf16[512,2048]{1,0:T(8,128)(2,1)} %collective-permute-done.22.refs_1_.refs_4_.refs_3_, bf16[512,2048]{1,0:T(8,128)(2,1)S(1)} %collective-permute-done.23.refs_2_.refs_5_.refs_4_, ...), custom_call_target="tpu_custom_call" | custom-call | bytes 1000000 | tf_op jit(solution)/shard_map/pallas_call | solution.py:137
  131.2 2.4 %collective-permute-start.31 = (bf16[512,2048]{1,0:T(8,128)(2,1)}, bf16[512,2048]{1,0:T(8,128)(2,1)S(1)}, u32[]{:S(2)}, u32[]{:S(2)}) collective-permute-start(bf16[512,2048]{1,0:T(8,128)(2,1)} %collective-permute-done.30.refs_2_.refs_5_.refs_7_), channel_id=1, source_target_pairs={{0,16},{16,32},{32,48},{48,0},{64,112},{80,64},{96,80},{112,96},{1... | collective-permute-start | bytes 6291464 | tf_op jit(solution)/shard_map/ppermute | solution.py:44
  136.2 4.7 %shard_map.105.mine_ref.mine_grad_ref = bf16[3,256,768]{2,1,0:T(8,128)(2,1)S(1)} custom-call(bf16[512,2048]{1,0:T(8,128)(2,1)} %collective-permute-done.24.refs_0_.refs_3_.refs_5_, bf16[512,2048]{1,0:T(8,128)(2,1)} %collective-permute-done.28.refs_1_.refs_4_.refs_6_, bf16[512,2048]{1,0:T(8,128)(2,1)} %collective-permute-done.30.refs_2_.refs_5_.refs_7_, ...), custom_call_target="tpu_custom_call" | custom-call | bytes 1000000 | tf_op jit(solution)/shard_map/pallas_call | solution.py:137
  141.1 2.8 %shard_map.106.refs_0_ = bf16[512,768]{1,0:T(8,128)(2,1)S(1)} custom-call(bf16[3,256,768]{2,1,0:T(8,128)(2,1)} %shard_map.100.mine_ref.mine_grad_ref, bf16[3,256,768]{2,1,0:T(8,128)(2,1)} %collective-permute-done.25.theirs_ref.theirs_grad_ref, bf16[3,256,768]{2,1,0:T(8,128)(2,1)} %shard_map.100.mine_ref.mine_grad_ref, ...), custom_call_target="tpu_custom_call" | custom-call | bytes 1000000 | tf_op jit(solution)/shard_map/pallas_call | solution.py:180
  143.9 2.4 %shard_map.108.refs_0_ = bf16[256,768]{1,0:T(8,128)(2,1)S(1)} custom-call(bf16[3,256,768]{2,1,0:T(8,128)(2,1)} %shard_map.100.mine_ref.mine_grad_ref, bf16[3,256,768]{2,1,0:T(8,128)(2,1)} %collective-permute-done.25.theirs_ref.theirs_grad_ref), custom_call_target="tpu_custom_call" | custom-call | bytes 1000000 | tf_op jit(solution)/shard_map/pallas_call | solution.py:180
  148.1 4.4 %shard_map.110.refs_8_ = f32[256,2048]{1,0:T(8,128)S(1)} custom-call(bf16[256,768]{1,0:T(8,128)(2,1)S(1)} %shard_map.108.refs_0_, bf16[256,768]{1,0:T(8,128)(2,1)S(1)} %shard_map.109.refs_1_, bf16[512,2048]{1,0:T(8,128)(2,1)S(1)} %shard_map.96.refs_0_.refs_3_.refs_2_, bf16[512,2048]{1,0:T(8,128)(2,1)S(1)} %shard_map.97.refs_1_.refs_4_.refs_3_, ...), custom_call_target="tpu_custom_call" | custom-call | bytes 1000000 | tf_op jit(solution)/shard_map/pallas_call | solution.py:240
  152.5 7.4 %shard_map.111.refs_8_ = f32[512,2048]{1,0:T(8,128)} custom-call(bf16[512,768]{1,0:T(8,128)(2,1)S(1)} %shard_map.106.refs_0_, bf16[512,768]{1,0:T(8,128)(2,1)S(1)} %shard_map.107.refs_1_, bf16[512,2048]{1,0:T(8,128)(2,1)S(1)} %shard_map.96.refs_0_.refs_3_.refs_2_, bf16[512,2048]{1,0:T(8,128)(2,1)S(1)} %shard_map.97.refs_1_.refs_4_.refs_3_, ...), custom_call_target="tpu_custom_call" | custom-call | bytes 1000000 | tf_op jit(solution)/shard_map/pallas_call | solution.py:240
  160.3 3.8 %shard_map.112.mine_ref = bf16[3,256,512]{2,1,0:T(8,128)(2,1)S(1)} custom-call(bf16[512,2048]{1,0:T(8,128)(2,1)} %collective-permute-done.27.refs_0_.refs_5_, bf16[512,2048]{1,0:T(8,128)(2,1)S(1)} %collective-permute-done.29.refs_1_.refs_6_, bf16[512,2048]{1,0:T(8,128)(2,1)S(1)} %collective-permute-done.31.refs_2_.refs_7_, ...), custom_call_target="tpu_custom_call" | custom-call | bytes 1000000 | tf_op jit(solution)/shard_map/pallas_call | solution.py:137
  165.4 2.5 %shard_map.116.mine_grad_ref = bf16[3,256,256]{2,1,0:T(8,128)(2,1)S(1)} custom-call(bf16[512,2048]{1,0:T(8,128)(2,1)} %collective-permute-done.27.refs_0_.refs_5_, bf16[512,2048]{1,0:T(8,128)(2,1)S(1)} %collective-permute-done.29.refs_1_.refs_6_, bf16[512,2048]{1,0:T(8,128)(2,1)S(1)} %collective-permute-done.31.refs_2_.refs_7_, bf16[256,2048]{1,0:T(8,128)(2,1)S(1)} %copy-done.8), custom_call_target="tpu_custom_call" | custom-call | bytes 1000000 | tf_op jit(solution)/shard_map/pallas_call | solution.py:137
  169.5 4.5 %shard_map.115 = bf16[16,224,128]{2,1,0:T(8,128)(2,1)S(1)} custom-call(bf16[256,768]{1,0:T(8,128)(2,1)S(1)} %shard_map.114.refs_0_, bf16[256,768]{1,0:T(8,128)(2,1)S(1)} %shard_map.113.refs_1_, bf16[512,2048]{1,0:T(8,128)(2,1)} %collective-permute-done.21.refs_0_.refs_3_.refs_2_, bf16[512,2048]{1,0:T(8,128)(2,1)} %collective-permute-done.22.refs_1_.refs_4_.refs_3_, ...), custom_call_target="tpu_custom_call" | custom-call | bytes 1000000 | tf_op jit(solution)/shard_map/pallas_call | solution.py:240
  176.7 4.6 %all-to-all-start = ((bf16[16,224,128]{2,1,0:T(8,128)(2,1)}), bf16[16,224,128]{2,1,0:T(8,128)(2,1)}, u32[]{:S(2)}, u32[]{:S(2)}) async-start(bf16[16,224,128]{2,1,0:T(8,128)(2,1)} %copy-done.24), calls=%async_computation | async-start | bytes 1835008 | tf_op jit(solution)/shard_map/all_to_all | solution.py:455
  184.1 2.7 %shard_map.117.refs_0_ = bf16[512,768]{1,0:T(8,128)(2,1)S(1)} custom-call(bf16[3,256,768]{2,1,0:T(8,128)(2,1)S(1)} %copy-done.11, bf16[3,256,512]{2,1,0:T(8,128)(2,1)S(1)} %copy-done.26, bf16[3,256,768]{2,1,0:T(8,128)(2,1)S(1)} %copy-done.11, bf16[3,256,256]{2,1,0:T(8,128)(2,1)} %collective-permute-done.37.theirs_grad_ref), custom_call_target="tpu_custom_call" | custom-call | bytes 1000000 | tf_op jit(solution)/shard_map/pallas_call | solution.py:180
  186.8 6.9 %shard_map.119 = (bf16[224,2048]{1,0:T(8,128)(2,1)}, bf16[224,2048]{1,0:T(8,128)(2,1)}) custom-call(bf16[512,768]{1,0:T(8,128)(2,1)S(1)} %shard_map.117.refs_0_, bf16[512,768]{1,0:T(8,128)(2,1)S(1)} %shard_map.118.refs_1_, bf16[512,2048]{1,0:T(8,128)(2,1)} %collective-permute-done.21.refs_0_.refs_3_.refs_2_, ...), custom_call_target="tpu_custom_call" | custom-call | bytes 1000000 | tf_op jit(solution)/shard_map/pallas_call | solution.py:240
  193.8 2.9 %collective-permute-done.36 = bf16[96,2048]{1,0:T(8,128)(2,1)} collective-permute-done((bf16[96,2048]{1,0:T(8,128)(2,1)}, bf16[96,2048]{1,0:T(8,128)(2,1)}, u32[]{:S(2)}, u32[]{:S(2)}) %collective-permute-start.36) | collective-permute-done | bytes 393248 | tf_op jit(solution)/shard_map/ppermute | solution.py:49
  196.7 2.3 %add_convert_fusion = (bf16[48,2048]{1,0:T(8,128)(2,1)}, bf16[48,2048]{1,0:T(8,128)(2,1)}) fusion(bf16[96,2048]{1,0:T(8,128)(2,1)} %collective-permute-done.36, bf16[96,2048]{1,0:T(8,128)(2,1)} %collective-permute-done.35, bf16[96,2048]{1,0:T(8,128)(2,1)} %collective-permute-done.34, bf16[96,2048]{1,0:T(8,128)(2,1)S(1)} %copy-done.42), kind=kLoop, calls=%fused_computation.8 | loop fusion | flops 1572864 | bytes 1966080 | tf_op jit(solution)/shard_map/convert_element_type | solution.py:333
  199.0 2.2 %copy.11 = bf16[3584,128]{1,0:T(8,128)(2,1)} copy(bf16[3584,128]{1,0:T(8,128)(2,1)} %bitcast.3) | data formatting | bytes 1835008
  (175 shorter events, 54.8 us)
Async XLA Ops:
  2.5 25.7 %collective-permute-start = (bf16[96,2048]{1,0:T(8,128)(2,1)S(1)}, bf16[96,2048]{1,0:T(8,128)(2,1)S(1)}, u32[]{:S(2)}, u32[]{:S(2)}) collective-permute-start(bf16[96,2048]{1,0:T(8,128)(2,1)S(1)} %get-tuple-element.69.refs_1_), channel_id=1, source_target_pairs={{0,16},{16,32},{32,48},{48,0},{1,17},{17,33},{33,49},{49,1},{2,18}... | collective-permute-start | bytes 1179656 | tf_op jit(solution)/shard_map/ppermute | solution.py:49
  4.6 23.6 %collective-permute-start.1 = (bf16[96,2048]{1,0:T(8,128)(2,1)S(1)}, bf16[96,2048]{1,0:T(8,128)(2,1)S(1)}, u32[]{:S(2)}, u32[]{:S(2)}) collective-permute-start(bf16[96,2048]{1,0:T(8,128)(2,1)S(1)} %get-tuple-element.69.refs_1_), channel_id=1, source_target_pairs={{0,32},{16,48},{32,0},{48,16},{1,33},{17,49},{33,1},{49,17},{2,34}... | collective-permute-start | bytes 1179656 | tf_op jit(solution)/shard_map/ppermute | solution.py:49
  7.1 21.1 %collective-permute-start.2 = (bf16[96,2048]{1,0:T(8,128)(2,1)S(1)}, bf16[96,2048]{1,0:T(8,128)(2,1)S(1)}, u32[]{:S(2)}, u32[]{:S(2)}) collective-permute-start(bf16[96,2048]{1,0:T(8,128)(2,1)S(1)} %get-tuple-element.69.refs_1_), channel_id=1, source_target_pairs={{0,48},{16,0},{32,16},{48,32},{1,49},{17,1},{33,17},{49,33},{2,50}... | collective-permute-start | bytes 1179656 | tf_op jit(solution)/shard_map/ppermute | solution.py:49
  8.3 9.6 %collective-permute-start.8 = (bf16[32,2048]{1,0:T(8,128)(2,1)S(1)}, bf16[32,2048]{1,0:T(8,128)(2,1)S(1)}, u32[]{:S(2)}, u32[]{:S(2)}) collective-permute-start(bf16[32,2048]{1,0:T(8,128)(2,1)S(1)} %get-tuple-element.74.refs_1_), channel_id=1, source_target_pairs={{0,1},{1,2},{2,3},{3,0},{4,5},{5,6},{6,7},{7,4},{8,9},{9,10},{10,1... | collective-permute-start | bytes 393224 | tf_op jit(solution)/shard_map/ppermute | solution.py:44
  11.0 7.4 %collective-permute-start.4 = (bf16[32,2048]{1,0:T(8,128)(2,1)S(1)}, bf16[32,2048]{1,0:T(8,128)(2,1)S(1)}, u32[]{:S(2)}, u32[]{:S(2)}) collective-permute-start(bf16[32,2048]{1,0:T(8,128)(2,1)S(1)} %get-tuple-element.73.refs_1_), channel_id=1, source_target_pairs={{0,4},{1,5},{2,6},{3,7},{4,8},{5,9},{6,10},{7,11},{8,12},{9,13},{1... | collective-permute-start | bytes 393224 | tf_op jit(solution)/shard_map/ppermute | solution.py:44
  27.9 9.5 %collective-permute-start.11 = (bf16[128,2048]{1,0:T(8,128)(2,1)S(1)}, bf16[128,2048]{1,0:T(8,128)(2,1)S(1)}, u32[]{:S(2)}, u32[]{:S(2)}) collective-permute-start(bf16[128,2048]{1,0:T(8,128)(2,1)S(1)} %shard_map.95.refs_1_), channel_id=1, source_target_pairs={{0,4},{1,5},{2,6},{3,7},{4,8},{5,9},{6,10},{7,11},{8,12},{9,13},{1... | collective-permute-start | bytes 1572872 | tf_op jit(solution)/shard_map/ppermute | solution.py:44
  28.1 9.2 %collective-permute-start.7 = (bf16[128,2048]{1,0:T(8,128)(2,1)S(1)}, bf16[128,2048]{1,0:T(8,128)(2,1)S(1)}, u32[]{:S(2)}, u32[]{:S(2)}) collective-permute-start(bf16[128,2048]{1,0:T(8,128)(2,1)S(1)} %shard_map.94.refs_1_), channel_id=1, source_target_pairs={{0,16},{16,32},{32,48},{48,0},{64,112},{80,64},{96,80},{112,96},{1... | collective-permute-start | bytes 1572872 | tf_op jit(solution)/shard_map/ppermute | solution.py:44
  28.4 9.0 %collective-permute-start.3 = (bf16[128,2048]{1,0:T(8,128)(2,1)S(1)}, bf16[128,2048]{1,0:T(8,128)(2,1)S(1)}, u32[]{:S(2)}, u32[]{:S(2)}) collective-permute-start(bf16[128,2048]{1,0:T(8,128)(2,1)S(1)} %get-tuple-element.82.refs_1_), channel_id=1, source_target_pairs={{0,1},{1,2},{2,3},{3,0},{4,5},{5,6},{6,7},{7,4},{8,9},{9,10},{10,1... | collective-permute-start | bytes 1572872 | tf_op jit(solution)/shard_map/ppermute | solution.py:44
  34.3 26.2 %collective-permute-start.16 = (bf16[192,3584]{1,0:T(8,128)(2,1)S(1)}, bf16[192,3584]{1,0:T(8,128)(2,1)S(1)}, u32[]{:S(2)}, u32[]{:S(2)}) collective-permute-start(bf16[192,3584]{1,0:T(8,128)(2,1)S(1)} %convolution_convert_fusion.2.refs_0_), channel_id=1, source_target_pairs={{0,64},{64,0},{1,65},{65,1},{2,66},{66,2},{3,67},{67,3},{4,68},{68... | collective-permute-start | bytes 4128776 | tf_op jit(solution)/shard_map/ppermute | solution.py:53
  37.4 15.2 %collective-permute-start.12 = (bf16[128,2048]{1,0:T(8,128)(2,1)S(1)}, bf16[128,2048]{1,0:T(8,128)(2,1)}, u32[]{:S(2)}, u32[]{:S(2)}) collective-permute-start(bf16[128,2048]{1,0:T(8,128)(2,1)S(1)} %collective-permute-done.3.refs_2_), channel_id=1, source_target_pairs={{0,1},{1,2},{2,3},{3,0},{4,5},{5,6},{6,7},{7,4},{8,9},{9,10},{10,1... | collective-permute-start | bytes 1572872 | tf_op jit(solution)/shard_map/ppermute | solution.py:44
  40.9 11.7 %collective-permute-start.13 = (bf16[128,2048]{1,0:T(8,128)(2,1)S(1)}, bf16[128,2048]{1,0:T(8,128)(2,1)S(1)}, u32[]{:S(2)}, u32[]{:S(2)}) collective-permute-start(bf16[128,2048]{1,0:T(8,128)(2,1)S(1)} %collective-permute-done.7.refs_2_), channel_id=1, source_target_pairs={{0,16},{16,32},{32,48},{48,0},{64,112},{80,64},{96,80},{112,96},{1... | collective-permute-start | bytes 1572872 | tf_op jit(solution)/shard_map/ppermute | solution.py:44
  40.9 11.7 %collective-permute-start.14 = (bf16[128,2048]{1,0:T(8,128)(2,1)S(1)}, bf16[128,2048]{1,0:T(8,128)(2,1)S(1)}, u32[]{:S(2)}, u32[]{:S(2)}) collective-permute-start(bf16[128,2048]{1,0:T(8,128)(2,1)S(1)} %collective-permute-done.11.refs_2_), channel_id=1, source_target_pairs={{0,4},{1,5},{2,6},{3,7},{4,8},{5,9},{6,10},{7,11},{8,12},{9,13},{1... | collective-permute-start | bytes 1572872 | tf_op jit(solution)/shard_map/ppermute | solution.py:44
  51.4 25.0 %collective-permute-start.17 = (bf16[192,3584]{1,0:T(8,128)(2,1)S(1)}, bf16[192,3584]{1,0:T(8,128)(2,1)}, u32[]{:S(2)}, u32[]{:S(2)}) collective-permute-start(bf16[192,3584]{1,0:T(8,128)(2,1)S(1)} %convolution_convert_fusion.1.refs_2_), channel_id=1, source_target_pairs={{0,64},{64,0},{1,65},{65,1},{2,66},{66,2},{3,67},{67,3},{4,68},{68... | collective-permute-start | bytes 4128776 | tf_op jit(solution)/shard_map/ppermute | solution.py:53
  52.6 20.3 %collective-permute-start.19 = (bf16[128,2048]{1,0:T(8,128)(2,1)S(1)}, bf16[128,2048]{1,0:T(8,128)(2,1)S(1)}, u32[]{:S(2)}, u32[]{:S(2)}) collective-permute-start(bf16[128,2048]{1,0:T(8,128)(2,1)S(1)} %collective-permute-done.14.refs_3_), channel_id=1, source_target_pairs={{0,4},{1,5},{2,6},{3,7},{4,8},{5,9},{6,10},{7,11},{8,12},{9,13},{1... | collective-permute-start | bytes 1572872 | tf_op jit(solution)/shard_map/ppermute | solution.py:44
  54.3 18.5 %collective-permute-start.18 = (bf16[128,2048]{1,0:T(8,128)(2,1)S(1)}, bf16[128,2048]{1,0:T(8,128)(2,1)S(1)}, u32[]{:S(2)}, u32[]{:S(2)}) collective-permute-start(bf16[128,2048]{1,0:T(8,128)(2,1)S(1)} %collective-permute-done.13.refs_3_), channel_id=1, source_target_pairs={{0,16},{16,32},{32,48},{48,0},{64,112},{80,64},{96,80},{112,96},{1... | collective-permute-start | bytes 1572872 | tf_op jit(solution)/shard_map/ppermute | solution.py:44
  58.1 18.2 %collective-permute-start.15 = (bf16[128,2048]{1,0:T(8,128)(2,1)}, bf16[128,2048]{1,0:T(8,128)(2,1)}, u32[]{:S(2)}, u32[]{:S(2)}) collective-permute-start(bf16[128,2048]{1,0:T(8,128)(2,1)} %collective-permute-done.12.refs_3_), channel_id=1, source_target_pairs={{0,1},{1,2},{2,3},{3,0},{4,5},{5,6},{6,7},{7,4},{8,9},{9,10},{10,1... | collective-permute-start | bytes 1572872 | tf_op jit(solution)/shard_map/ppermute | solution.py:44
  73.8 27.2 %collective-permute-start.23 = (bf16[512,2048]{1,0:T(8,128)(2,1)S(1)}, bf16[512,2048]{1,0:T(8,128)(2,1)S(1)}, u32[]{:S(2)}, u32[]{:S(2)}) collective-permute-start(bf16[512,2048]{1,0:T(8,128)(2,1)S(1)} %shard_map.98.refs_2_.refs_5_.refs_4_), channel_id=1, source_target_pairs={{0,16},{16,32},{32,48},{48,0},{64,112},{80,64},{96,80},{112,96},{1... | collective-permute-start | bytes 6291464 | tf_op jit(solution)/shard_map/ppermute | solution.py:44
  76.2 25.4 %collective-permute-start.22 = (bf16[512,2048]{1,0:T(8,128)(2,1)S(1)}, bf16[512,2048]{1,0:T(8,128)(2,1)}, u32[]{:S(2)}, u32[]{:S(2)}) collective-permute-start(bf16[512,2048]{1,0:T(8,128)(2,1)S(1)} %shard_map.97.refs_1_.refs_4_.refs_3_), channel_id=1, source_target_pairs={{0,1},{1,2},{2,3},{3,0},{4,5},{5,6},{6,7},{7,4},{8,9},{9,10},{10,1... | collective-permute-start | bytes 6291464 | tf_op jit(solution)/shard_map/ppermute | solution.py:44
  77.7 25.1 %collective-permute-start.21 = (bf16[512,2048]{1,0:T(8,128)(2,1)S(1)}, bf16[512,2048]{1,0:T(8,128)(2,1)}, u32[]{:S(2)}, u32[]{:S(2)}) collective-permute-start(bf16[512,2048]{1,0:T(8,128)(2,1)S(1)} %shard_map.96.refs_0_.refs_3_.refs_2_), channel_id=1, source_target_pairs={{0,4},{1,5},{2,6},{3,7},{4,8},{5,9},{6,10},{7,11},{8,12},{9,13},{1... | collective-permute-start | bytes 6291464 | tf_op jit(solution)/shard_map/ppermute | solution.py:44
  77.9 14.8 %collective-permute-start.20 = (bf16[192,3584]{1,0:T(8,128)(2,1)}, bf16[192,3584]{1,0:T(8,128)(2,1)}, u32[]{:S(2)}, u32[]{:S(2)}) collective-permute-start(bf16[192,3584]{1,0:T(8,128)(2,1)} %convolution_convert_fusion.refs_4_), channel_id=1, source_target_pairs={{0,64},{64,0},{1,65},{65,1},{2,66},{66,2},{3,67},{67,3},{4,68},{68... | collective-permute-start | bytes 4128776 | tf_op jit(solution)/shard_map/ppermute | solution.py:53
  101.0 30.2 %collective-permute-start.30 = (bf16[512,2048]{1,0:T(8,128)(2,1)S(1)}, bf16[512,2048]{1,0:T(8,128)(2,1)}, u32[]{:S(2)}, u32[]{:S(2)}) collective-permute-start(bf16[512,2048]{1,0:T(8,128)(2,1)S(1)} %collective-permute-done.23.refs_2_.refs_5_.refs_4_), channel_id=1, source_target_pairs={{0,16},{16,32},{32,48},{48,0},{64,112},{80,64},{96,80},{112,96},{1... | collective-permute-start | bytes 6291464 | tf_op jit(solution)/shard_map/ppermute | solution.py:44
  101.6 32.0 %collective-permute-start.28 = (bf16[512,2048]{1,0:T(8,128)(2,1)}, bf16[512,2048]{1,0:T(8,128)(2,1)}, u32[]{:S(2)}, u32[]{:S(2)}) collective-permute-start(bf16[512,2048]{1,0:T(8,128)(2,1)} %collective-permute-done.22.refs_1_.refs_4_.refs_3_), channel_id=1, source_target_pairs={{0,1},{1,2},{2,3},{3,0},{4,5},{5,6},{6,7},{7,4},{8,9},{9,10},{10,1... | collective-permute-start | bytes 6291464 | tf_op jit(solution)/shard_map/ppermute | solution.py:44
  102.8 32.0 %collective-permute-start.24 = (bf16[512,2048]{1,0:T(8,128)(2,1)}, bf16[512,2048]{1,0:T(8,128)(2,1)}, u32[]{:S(2)}, u32[]{:S(2)}) collective-permute-start(bf16[512,2048]{1,0:T(8,128)(2,1)} %collective-permute-done.21.refs_0_.refs_3_.refs_2_), channel_id=1, source_target_pairs={{0,4},{1,5},{2,6},{3,7},{4,8},{5,9},{6,10},{7,11},{8,12},{9,13},{1... | collective-permute-start | bytes 6291464 | tf_op jit(solution)/shard_map/ppermute | solution.py:44
  104.2 25.0 %collective-permute-start.25 = (bf16[3,256,768]{2,1,0:T(8,128)(2,1)}, bf16[3,256,768]{2,1,0:T(8,128)(2,1)}, u32[]{:S(2)}, u32[]{:S(2)}) collective-permute-start(bf16[3,256,768]{2,1,0:T(8,128)(2,1)} %shard_map.100.mine_ref.mine_grad_ref), channel_id=1, source_target_pairs={{0,64},{64,0},{1,65},{65,1},{2,66},{66,2},{3,67},{67,3},{4,68},{68... | collective-permute-start | bytes 3538952 | tf_op jit(solution)/shard_map/ppermute | solution.py:53
  131.2 28.7 %collective-permute-start.31 = (bf16[512,2048]{1,0:T(8,128)(2,1)}, bf16[512,2048]{1,0:T(8,128)(2,1)S(1)}, u32[]{:S(2)}, u32[]{:S(2)}) collective-permute-start(bf16[512,2048]{1,0:T(8,128)(2,1)} %collective-permute-done.30.refs_2_.refs_5_.refs_7_), channel_id=1, source_target_pairs={{0,16},{16,32},{32,48},{48,0},{64,112},{80,64},{96,80},{112,96},{1... | collective-permute-start | bytes 6291464 | tf_op jit(solution)/shard_map/ppermute | solution.py:44
  133.6 26.4 %collective-permute-start.29 = (bf16[512,2048]{1,0:T(8,128)(2,1)}, bf16[512,2048]{1,0:T(8,128)(2,1)S(1)}, u32[]{:S(2)}, u32[]{:S(2)}) collective-permute-start(bf16[512,2048]{1,0:T(8,128)(2,1)} %collective-permute-done.28.refs_1_.refs_4_.refs_6_), channel_id=1, source_target_pairs={{0,1},{1,2},{2,3},{3,0},{4,5},{5,6},{6,7},{7,4},{8,9},{9,10},{10,1... | collective-permute-start | bytes 6291464 | tf_op jit(solution)/shard_map/ppermute | solution.py:44
  134.8 25.5 %collective-permute-start.27 = (bf16[512,2048]{1,0:T(8,128)(2,1)}, bf16[512,2048]{1,0:T(8,128)(2,1)}, u32[]{:S(2)}, u32[]{:S(2)}) collective-permute-start(bf16[512,2048]{1,0:T(8,128)(2,1)} %collective-permute-done.24.refs_0_.refs_3_.refs_5_), channel_id=1, source_target_pairs={{0,4},{1,5},{2,6},{3,7},{4,8},{5,9},{6,10},{7,11},{8,12},{9,13},{1... | collective-permute-start | bytes 6291464 | tf_op jit(solution)/shard_map/ppermute | solution.py:44
  167.8 15.8 %collective-permute-start.37 = (bf16[3,256,256]{2,1,0:T(8,128)(2,1)S(1)}, bf16[3,256,256]{2,1,0:T(8,128)(2,1)}, u32[]{:S(2)}, u32[]{:S(2)}) collective-permute-start(bf16[3,256,256]{2,1,0:T(8,128)(2,1)S(1)} %shard_map.116.mine_grad_ref), channel_id=1, source_target_pairs={{0,64},{64,0},{1,65},{65,1},{2,66},{66,2},{3,67},{67,3},{4,68},{68... | collective-permute-start | bytes 1179656 | tf_op jit(solution)/shard_map/ppermute | solution.py:53
  174.1 19.7 %collective-permute-start.34 = (bf16[96,2048]{1,0:T(8,128)(2,1)}, bf16[96,2048]{1,0:T(8,128)(2,1)}, u32[]{:S(2)}, u32[]{:S(2)}) collective-permute-start(bf16[96,2048]{1,0:T(8,128)(2,1)} %get-tuple-element.123), channel_id=1, source_target_pairs={{0,48},{16,0},{32,16},{48,32},{1,49},{17,1},{33,17},{49,33},{2,50}... | collective-permute-start | bytes 1179656 | tf_op jit(solution)/shard_map/ppermute | solution.py:49
  176.0 17.8 %collective-permute-start.35 = (bf16[96,2048]{1,0:T(8,128)(2,1)}, bf16[96,2048]{1,0:T(8,128)(2,1)}, u32[]{:S(2)}, u32[]{:S(2)}) collective-permute-start(bf16[96,2048]{1,0:T(8,128)(2,1)} %get-tuple-element.124), channel_id=1, source_target_pairs={{0,32},{16,48},{32,0},{48,16},{1,33},{17,49},{33,1},{49,17},{2,34}... | collective-permute-start | bytes 1179656 | tf_op jit(solution)/shard_map/ppermute | solution.py:49
  176.0 20.6 %collective-permute-start.36 = (bf16[96,2048]{1,0:T(8,128)(2,1)}, bf16[96,2048]{1,0:T(8,128)(2,1)}, u32[]{:S(2)}, u32[]{:S(2)}) collective-permute-start(bf16[96,2048]{1,0:T(8,128)(2,1)} %get-tuple-element.125), channel_id=1, source_target_pairs={{0,16},{16,32},{32,48},{48,0},{1,17},{17,33},{33,49},{49,1},{2,18}... | collective-permute-start | bytes 1179656 | tf_op jit(solution)/shard_map/ppermute | solution.py:49
  176.7 22.3 %all-to-all-start = ((bf16[16,224,128]{2,1,0:T(8,128)(2,1)}), bf16[16,224,128]{2,1,0:T(8,128)(2,1)}, u32[]{:S(2)}, u32[]{:S(2)}) async-start(bf16[16,224,128]{2,1,0:T(8,128)(2,1)} %copy-done.24), calls=%async_computation | async-start | bytes 1835008 | tf_op jit(solution)/shard_map/all_to_all | solution.py:455
  (53 other events, 257.7 us)
where the time goes:
time: 202 us; the launch traced here: 201 us
  Pallas kernels  89.2 us (44%)
  starting transfers between devices  56.1 us (28%)
  local copies, waits for them, and re-layouts  22.5 us (11%)
  matrix products  22.4 us (11%)
  waiting for transfers between devices  6.95 us (3%)
  other arithmetic  2.65 us (1%)
    ppermute x24, starting transfers between devices, hop(): return lax.ppermute(array, ('row', mesh_axis(axis)), pairs)  37.8 us
    pallas_call x4, Pallas kernels, weight_grad(): pl.pallas_call(lambda *refs: weight_grad_kernel(n_groups, n_parts, before...  23.3 us
    pallas_call x5, Pallas kernels, own_partials(): pl.pallas_call(lambda *refs: own_partials_kernel(n_parts, sides, *refs),...  19 us
    unnamed x93, local copies, waits for them, and re-layouts  17 us
    pallas_call x1, Pallas kernels, input_product(): pl.pallas_call(input_kernel, grid=(features // block,), in_specs=[*map(wh...  16.2 us
    pallas_call x8, Pallas kernels, activations(): pl.pallas_call(kernel, grid=(n_parts,), in_specs=[spec(columns, block) fo...  11.9 us
    dot_general x1, matrix products, times_transpose(): return lax.dot_general(left, right, LAST, preferred_element_type=F32)  11.2 us
    dot_general x2, matrix products, plain(): return jnp.dot(left, right, preferred_element_type=F32)  11.2 us
  transfers between devices with their start and end apart: 39, of which 5 were waited for; matrix products, arithmetic and copies ran while one was open for 15% of the time, Pallas kernels for 42%

commit v1 on v0

--- a/solution.py
+++ b/solution.py
@@ -248,6 +248,28 @@
     )(*args)
 
 
+def transposed_kernel(left_ref, weight_ref, out_ref):
+    out_ref[...] = times_transpose(left_ref[...], weight_ref[...]).astype(BF16)
+
+
+def transposed_product(left, weight, block=896):
+    width, features = weight.shape
+    tokens = left.shape[0]
+    return pl.pallas_call(
+        transposed_kernel,
+        grid=(width // block,),
+        in_specs=[whole(left), pl.BlockSpec((block, features), lambda i: (i, 0))],
+        out_specs=pl.BlockSpec((tokens, block), lambda i: (0, i)),
+        out_shape=jax.ShapeDtypeStruct((tokens, width), BF16),
+        cost_estimate=pl.CostEstimate(
+            flops=8 * tokens * width * features,
+            bytes_accessed=8 * width * features,
+            transcendentals=0,
+        ),
+        compiler_params=pltpu.CompilerParams(vmem_limit_bytes=24 * MIB),
+    )(left, weight)
+
+
 def sums_at(refs, columns):
     return [
         mine[:, columns].astype(F32) + theirs[:, columns].astype(F32)
@@ -385,7 +407,7 @@
     (r2_, t2_, q2_) = tie((r2, t2, q2), up_part)
     r3, t3, q3 = hop(r2_, "y"), hop(t2_, "x"), hop(q2_, "z")
     up_theirs = swap(up_part)
-    grad_part = times_transpose(grad_panel, down_weight).astype(BF16)
+    grad_part = transposed_product(grad_panel, down_weight)
 
     r0, r1, r2, r3 = tie((r0, r1, r2, r3), grad_part, up_theirs)
     t0, t1, t2, t3 = tie((t0, t1, t2, t3), grad_part)

time: 202 us -> 196 us (0.970)
  matrix products: 22.4 us -> 16.5 us
  Pallas kernels: 89.2 us -> 93.8 us
  local copies, waits for them, and re-layouts: 22.5 us -> 19.5 us
    dot_general x1 -> x0, matrix products: 11.2 us -> none  [times_transpose(): return lax.dot_general(left, right, LAST, preferred_element_type=F32)]
    pallas_call x0 -> x1, Pallas kernels: none -> 6.23 us  [transposed_product(): pl.pallas_call(transposed_kernel, grid=(width // block,), in_specs=[whole...]
    dot_general x2, matrix products: 11.2 us -> 16.5 us  [plain(): return jnp.dot(left, right, preferred_element_type=F32)]
    unnamed x93 -> x79, local copies, waits for them, and re-layouts: 17 us -> 14.1 us
  transfers between devices with their start and end apart: 39 -> 39, of which waited for: 5 -> 3; matrix products, arithmetic and copies ran while one was open for 15% -> 13% of each run, Pallas kernels for 42% -> 46%
where the time goes in v1:
time: 196 us; the launch traced here: 195 us
  Pallas kernels  93.8 us (48%)
  starting transfers between devices  55.8 us (28%)
  local copies, waits for them, and re-layouts  19.5 us (10%)
  matrix products  16.5 us (8%)
  waiting for transfers between devices  5.41 us (3%)
  other arithmetic  2.65 us (1%)
    ppermute x24, starting transfers between devices, hop(): return lax.ppermute(array, ('row', mesh_axis(axis)), pairs)  39.2 us
    pallas_call x4, Pallas kernels, weight_grad(): pl.pallas_call(lambda *refs: weight_grad_kernel(n_groups, n_parts, before...  23.3 us
    pallas_call x5, Pallas kernels, own_partials(): pl.pallas_call(lambda *refs: own_partials_kernel(n_parts, sides, *refs),...  18.9 us
    dot_general x2, matrix products, plain(): return jnp.dot(left, right, preferred_element_type=F32)  16.5 us
    pallas_call x1, Pallas kernels, input_product(): pl.pallas_call(input_kernel, grid=(features // block,), in_specs=[*map(wh...  16.2 us
    unnamed x79, local copies, waits for them, and re-layouts  14.1 us
    pallas_call x8, Pallas kernels, activations(): pl.pallas_call(kernel, grid=(n_parts,), in_specs=[spec(columns, block) fo...  11.9 us
    pallas_call x1, Pallas kernels, mixed_product(): pl.pallas_call(mixed_kernel, grid=(features // block,), in_specs=[*map(wh...  9.82 us
  transfers between devices with their start and end apart: 39, of which 3 were waited for; matrix products, arithmetic and copies ran while one was open for 13% of the time, Pallas kernels for 46%

profile of v1, /device:TPU:1, one launch (start us, length us, event | category | flops | bytes accessed | tf_op | source)
XLA Modules:
  0.0 195.0 jit_solution(11817700822615408283)
XLA Ops:
  4.6 2.5 %collective-permute-start.1 = (bf16[96,2048]{1,0:T(8,128)(2,1)S(1)}, bf16[96,2048]{1,0:T(8,128)(2,1)S(1)}, u32[]{:S(2)}, u32[]{:S(2)}) collective-permute-start(bf16[96,2048]{1,0:T(8,128)(2,1)S(1)} %get-tuple-element.69.refs_1_), channel_id=1, source_target_pairs={{0,32},{16,48},{32,0},{48,16},{1,33},{17,49},{33,1},{49,17},{2,34}... | collective-permute-start | bytes 1179656 | tf_op jit(solution)/shard_map/ppermute | solution.py:49
  8.3 2.7 %collective-permute-start.8 = (bf16[32,2048]{1,0:T(8,128)(2,1)S(1)}, bf16[32,2048]{1,0:T(8,128)(2,1)S(1)}, u32[]{:S(2)}, u32[]{:S(2)}) collective-permute-start(bf16[32,2048]{1,0:T(8,128)(2,1)S(1)} %get-tuple-element.74.refs_1_), channel_id=1, source_target_pairs={{0,1},{1,2},{2,3},{3,0},{4,5},{5,6},{6,7},{7,4},{8,9},{9,10},{10,1... | collective-permute-start | bytes 393224 | tf_op jit(solution)/shard_map/ppermute | solution.py:44
  11.0 3.8 %collective-permute-start.4 = (bf16[32,2048]{1,0:T(8,128)(2,1)S(1)}, bf16[32,2048]{1,0:T(8,128)(2,1)S(1)}, u32[]{:S(2)}, u32[]{:S(2)}) collective-permute-start(bf16[32,2048]{1,0:T(8,128)(2,1)S(1)} %get-tuple-element.73.refs_1_), channel_id=1, source_target_pairs={{0,4},{1,5},{2,6},{3,7},{4,8},{5,9},{6,10},{7,11},{8,12},{9,13},{1... | collective-permute-start | bytes 393224 | tf_op jit(solution)/shard_map/ppermute | solution.py:44
  14.7 2.9 %constant_dynamic-slice_fusion.1 = (bf16[2048,224]{1,0:T(8,128)(2,1)S(1)}, bf16[2048,224]{1,0:T(8,128)(2,1)S(1)}) fusion(bf16[2048,3584]{1,0:T(8,128)(2,1)} %up_ref.1, s32[]{:T(128)S(6)} %select_n.2, bf16[2048,3584]{1,0:T(8,128)(2,1)} %gate_ref.1), kind=kLoop, calls=%fused_computation.10 | loop fusion | bytes 3670020 | tf_op jit(solution)/shard_map/dynamic_slice | solution.py:389
  28.4 2.8 %collective-permute-start.3 = (bf16[128,2048]{1,0:T(8,128)(2,1)S(1)}, bf16[128,2048]{1,0:T(8,128)(2,1)S(1)}, u32[]{:S(2)}, u32[]{:S(2)}) collective-permute-start(bf16[128,2048]{1,0:T(8,128)(2,1)S(1)} %get-tuple-element.82.refs_1_), channel_id=1, source_target_pairs={{0,1},{1,2},{2,3},{3,0},{4,5},{5,6},{6,7},{7,4},{8,9},{9,10},{10,1... | collective-permute-start | bytes 1572872 | tf_op jit(solution)/shard_map/ppermute | solution.py:44
  31.2 8.3 %convolution_convert_fusion.1.refs_0_ = bf16[192,3584]{1,0:T(8,128)(2,1)S(1)} fusion(bf16[192,2048]{1,0:T(8,128)(2,1)S(1)} %get-tuple-element.78, bf16[2048,3584]{1,0:T(8,128)(2,1)} %gate_ref.1), kind=kOutput, calls=%fused_computation.1 | convolution fusion | flops 2819260416 | bytes 16842752 | tf_op jit(solution)/shard_map/dot_general | solution.py:100
  43.1 2.4 %collective-permute-start.13 = (bf16[128,2048]{1,0:T(8,128)(2,1)S(1)}, bf16[128,2048]{1,0:T(8,128)(2,1)S(1)}, u32[]{:S(2)}, u32[]{:S(2)}) collective-permute-start(bf16[128,2048]{1,0:T(8,128)(2,1)S(1)} %collective-permute-done.7.refs_2_), channel_id=1, source_target_pairs={{0,16},{16,32},{32,48},{48,0},{64,112},{80,64},{96,80},{112,96},{1... | collective-permute-start | bytes 1572872 | tf_op jit(solution)/shard_map/ppermute | solution.py:44
  47.0 8.2 %convolution_convert_fusion.refs_2_ = bf16[192,3584]{1,0:T(8,128)(2,1)S(1)} fusion(bf16[192,2048]{1,0:T(8,128)(2,1)S(1)} %get-tuple-element.78, bf16[2048,3584]{1,0:T(8,128)(2,1)} %up_ref.1), kind=kOutput, calls=%fused_computation | convolution fusion | flops 2819260416 | bytes 16842752 | tf_op jit(solution)/shard_map/dot_general | solution.py:100
  59.5 6.2 %shard_map.96.refs_4_ = bf16[192,3584]{1,0:T(8,128)(2,1)} custom-call(bf16[192,2048]{1,0:T(8,128)(2,1)S(1)} %get-tuple-element.81.left_ref, bf16[3584,2048]{1,0:T(8,128)(2,1)S(1)} %bitcast.9), custom_call_target="tpu_custom_call" | custom-call | flops 11274289152 | bytes 58720256 | tf_op jit(solution)/shard_map/pallas_call | solution.py:258
  70.5 9.8 %shard_map.100.refs_1_ = bf16[192,2048]{1,0:T(8,128)(2,1)S(1)} custom-call(bf16[192,3584]{1,0:T(8,128)(2,1)} %copy-done.18, bf16[192,3584]{1,0:T(8,128)(2,1)} %copy-done.20, bf16[192,3584]{1,0:T(8,128)(2,1)} %copy-done.22, bf16[192,3584]{1,0:T(8,128)(2,1)} %copy-done.24, bf16[3584,2048]{1,0:T(8,128)(2,1)} %refs_4_.1), custom_call_target="tpu_custom_call" | custom-call | bytes 1000000 | tf_op jit(solution)/shard_map/pallas_call | solution.py:300
  81.6 3.7 %shard_map.101.mine_ref.mine_grad_ref = bf16[3,256,768]{2,1,0:T(8,128)(2,1)} custom-call(bf16[512,2048]{1,0:T(8,128)(2,1)S(1)} %shard_map.97.refs_0_.refs_3_.refs_2_, bf16[512,2048]{1,0:T(8,128)(2,1)S(1)} %shard_map.98.refs_1_.refs_4_.refs_3_, bf16[512,2048]{1,0:T(8,128)(2,1)S(1)} %shard_map.99.refs_2_.refs_5_.refs_4_, ...), custom_call_target="tpu_custom_call" | custom-call | bytes 1000000 | tf_op jit(solution)/shard_map/pallas_call | solution.py:137
  85.3 5.6 %shard_map.102 = (bf16[192,3584]{1,0:T(8,128)(2,1)S(1)}, bf16[192,3584]{1,0:T(8,128)(2,1)S(1)}) custom-call(bf16[192,3584]{1,0:T(8,128)(2,1)S(1)} %copy-done.19, bf16[192,3584]{1,0:T(8,128)(2,1)S(1)} %copy-done.21, bf16[192,3584]{1,0:T(8,128)(2,1)S(1)} %copy-done.23, bf16[192,3584]{1,0:T(8,128)(2,1)S(1)} %copy-done.25, bf16[192,3584]{1,0:T(8,128)(2,1)} %shard_map.96.refs_4_, ...), custom_call_target="tpu_custom_call" | custom-call | bytes 1000000 | tf_op jit(solution)/shard_map/pallas_call | solution.py:319
  93.1 2.3 %collective-permute-start.30 = (bf16[512,2048]{1,0:T(8,128)(2,1)S(1)}, bf16[512,2048]{1,0:T(8,128)(2,1)}, u32[]{:S(2)}, u32[]{:S(2)}) collective-permute-start(bf16[512,2048]{1,0:T(8,128)(2,1)S(1)} %collective-permute-done.23.refs_2_.refs_5_.refs_4_), channel_id=1, source_target_pairs={{0,16},{16,32},{32,48},{48,0},{64,112},{80,64},{96,80},{112,96},{1... | collective-permute-start | bytes 6291464 | tf_op jit(solution)/shard_map/ppermute | solution.py:44
  95.4 2.9 %collective-permute-start.28 = (bf16[512,2048]{1,0:T(8,128)(2,1)}, bf16[512,2048]{1,0:T(8,128)(2,1)}, u32[]{:S(2)}, u32[]{:S(2)}) collective-permute-start(bf16[512,2048]{1,0:T(8,128)(2,1)} %collective-permute-done.22.refs_1_.refs_4_.refs_3_), channel_id=1, source_target_pairs={{0,1},{1,2},{2,3},{3,0},{4,5},{5,6},{6,7},{7,4},{8,9},{9,10},{10,1... | collective-permute-start | bytes 6291464 | tf_op jit(solution)/shard_map/ppermute | solution.py:44
  99.7 16.2 %shard_map.103.refs_2_ = bf16[192,2048]{1,0:T(8,128)(2,1)S(1)} custom-call(bf16[192,3584]{1,0:T(8,128)(2,1)} %copy-done.29, bf16[192,3584]{1,0:T(8,128)(2,1)} %copy-done.30, bf16[2048,3584]{1,0:T(8,128)(2,1)} %gate_ref.1, bf16[2048,3584]{1,0:T(8,128)(2,1)} %up_ref.1), custom_call_target="tpu_custom_call" | custom-call | bytes 1000000 | tf_op jit(solution)/shard_map/pallas_call | solution.py:340
  117.2 4.4 %shard_map.105.mine_ref.mine_grad_ref = bf16[3,256,768]{2,1,0:T(8,128)(2,1)S(1)} custom-call(bf16[512,2048]{1,0:T(8,128)(2,1)} %collective-permute-done.21.refs_0_.refs_3_.refs_2_, bf16[512,2048]{1,0:T(8,128)(2,1)} %collective-permute-done.22.refs_1_.refs_4_.refs_3_, bf16[512,2048]{1,0:T(8,128)(2,1)S(1)} %collective-permute-done.23.refs_2_.refs_5_.refs_4_, ...), custom_call_target="tpu_custom_call" | custom-call | bytes 1000000 | tf_op jit(solution)/shard_map/pallas_call | solution.py:137
  127.8 2.4 %collective-permute-start.27 = (bf16[512,2048]{1,0:T(8,128)(2,1)}, bf16[512,2048]{1,0:T(8,128)(2,1)}, u32[]{:S(2)}, u32[]{:S(2)}) collective-permute-start(bf16[512,2048]{1,0:T(8,128)(2,1)} %collective-permute-done.24.refs_0_.refs_3_.refs_5_), channel_id=1, source_target_pairs={{0,4},{1,5},{2,6},{3,7},{4,8},{5,9},{6,10},{7,11},{8,12},{9,13},{1... | collective-permute-start | bytes 6291464 | tf_op jit(solution)/shard_map/ppermute | solution.py:44
  130.3 4.7 %shard_map.106.mine_ref.mine_grad_ref = bf16[3,256,768]{2,1,0:T(8,128)(2,1)S(1)} custom-call(bf16[512,2048]{1,0:T(8,128)(2,1)} %collective-permute-done.24.refs_0_.refs_3_.refs_5_, bf16[512,2048]{1,0:T(8,128)(2,1)} %collective-permute-done.28.refs_1_.refs_4_.refs_6_, bf16[512,2048]{1,0:T(8,128)(2,1)} %collective-permute-done.30.refs_2_.refs_5_.refs_7_, ...), custom_call_target="tpu_custom_call" | custom-call | bytes 1000000 | tf_op jit(solution)/shard_map/pallas_call | solution.py:137
  135.1 2.8 %shard_map.107.refs_0_ = bf16[512,768]{1,0:T(8,128)(2,1)S(1)} custom-call(bf16[3,256,768]{2,1,0:T(8,128)(2,1)} %shard_map.101.mine_ref.mine_grad_ref, bf16[3,256,768]{2,1,0:T(8,128)(2,1)} %collective-permute-done.25.theirs_ref.theirs_grad_ref, bf16[3,256,768]{2,1,0:T(8,128)(2,1)} %shard_map.101.mine_ref.mine_grad_ref, ...), custom_call_target="tpu_custom_call" | custom-call | bytes 1000000 | tf_op jit(solution)/shard_map/pallas_call | solution.py:180
  137.9 2.4 %shard_map.109.refs_0_ = bf16[256,768]{1,0:T(8,128)(2,1)S(1)} custom-call(bf16[3,256,768]{2,1,0:T(8,128)(2,1)} %shard_map.101.mine_ref.mine_grad_ref, bf16[3,256,768]{2,1,0:T(8,128)(2,1)} %collective-permute-done.25.theirs_ref.theirs_grad_ref), custom_call_target="tpu_custom_call" | custom-call | bytes 1000000 | tf_op jit(solution)/shard_map/pallas_call | solution.py:180
  142.1 4.4 %shard_map.111.refs_8_ = f32[256,2048]{1,0:T(8,128)S(1)} custom-call(bf16[256,768]{1,0:T(8,128)(2,1)S(1)} %shard_map.109.refs_0_, bf16[256,768]{1,0:T(8,128)(2,1)S(1)} %shard_map.110.refs_1_, bf16[512,2048]{1,0:T(8,128)(2,1)S(1)} %shard_map.97.refs_0_.refs_3_.refs_2_, bf16[512,2048]{1,0:T(8,128)(2,1)S(1)} %shard_map.98.refs_1_.refs_4_.refs_3_, ...), custom_call_target="tpu_custom_call" | custom-call | bytes 1000000 | tf_op jit(solution)/shard_map/pallas_call | solution.py:240
  146.5 7.5 %shard_map.112.refs_8_ = f32[512,2048]{1,0:T(8,128)} custom-call(bf16[512,768]{1,0:T(8,128)(2,1)S(1)} %shard_map.107.refs_0_, bf16[512,768]{1,0:T(8,128)(2,1)S(1)} %shard_map.108.refs_1_, bf16[512,2048]{1,0:T(8,128)(2,1)S(1)} %shard_map.97.refs_0_.refs_3_.refs_2_, bf16[512,2048]{1,0:T(8,128)(2,1)S(1)} %shard_map.98.refs_1_.refs_4_.refs_3_, ...), custom_call_target="tpu_custom_call" | custom-call | bytes 1000000 | tf_op jit(solution)/shard_map/pallas_call | solution.py:240
  154.1 3.6 %shard_map.113.mine_ref = bf16[3,256,512]{2,1,0:T(8,128)(2,1)S(1)} custom-call(bf16[512,2048]{1,0:T(8,128)(2,1)} %collective-permute-done.27.refs_0_.refs_5_, bf16[512,2048]{1,0:T(8,128)(2,1)S(1)} %collective-permute-done.29.refs_1_.refs_6_, bf16[512,2048]{1,0:T(8,128)(2,1)S(1)} %collective-permute-done.31.refs_2_.refs_7_, ...), custom_call_target="tpu_custom_call" | custom-call | bytes 1000000 | tf_op jit(solution)/shard_map/pallas_call | solution.py:137
  158.9 2.5 %shard_map.117.mine_grad_ref = bf16[3,256,256]{2,1,0:T(8,128)(2,1)S(1)} custom-call(bf16[512,2048]{1,0:T(8,128)(2,1)} %collective-permute-done.27.refs_0_.refs_5_, bf16[512,2048]{1,0:T(8,128)(2,1)S(1)} %collective-permute-done.29.refs_1_.refs_6_, bf16[512,2048]{1,0:T(8,128)(2,1)S(1)} %collective-permute-done.31.refs_2_.refs_7_, bf16[256,2048]{1,0:T(8,128)(2,1)S(1)} %copy-done.8), custom_call_target="tpu_custom_call" | custom-call | bytes 1000000 | tf_op jit(solution)/shard_map/pallas_call | solution.py:137
  163.1 4.5 %shard_map.116 = bf16[16,224,128]{2,1,0:T(8,128)(2,1)S(1)} custom-call(bf16[256,768]{1,0:T(8,128)(2,1)S(1)} %shard_map.115.refs_0_, bf16[256,768]{1,0:T(8,128)(2,1)S(1)} %shard_map.114.refs_1_, bf16[512,2048]{1,0:T(8,128)(2,1)} %collective-permute-done.21.refs_0_.refs_3_.refs_2_, bf16[512,2048]{1,0:T(8,128)(2,1)} %collective-permute-done.22.refs_1_.refs_4_.refs_3_, ...), custom_call_target="tpu_custom_call" | custom-call | bytes 1000000 | tf_op jit(solution)/shard_map/pallas_call | solution.py:240
  167.6 2.2 %collective-permute-start.34 = (bf16[96,2048]{1,0:T(8,128)(2,1)}, bf16[96,2048]{1,0:T(8,128)(2,1)}, u32[]{:S(2)}, u32[]{:S(2)}) collective-permute-start(bf16[96,2048]{1,0:T(8,128)(2,1)} %get-tuple-element.123), channel_id=1, source_target_pairs={{0,48},{16,0},{32,16},{48,32},{1,49},{17,1},{33,17},{49,33},{2,50}... | collective-permute-start | bytes 1179656 | tf_op jit(solution)/shard_map/ppermute | solution.py:49
  170.5 4.3 %all-to-all-start = ((bf16[16,224,128]{2,1,0:T(8,128)(2,1)}), bf16[16,224,128]{2,1,0:T(8,128)(2,1)}, u32[]{:S(2)}, u32[]{:S(2)}) async-start(bf16[16,224,128]{2,1,0:T(8,128)(2,1)} %copy-done.26), calls=%async_computation | async-start | bytes 1835008 | tf_op jit(solution)/shard_map/all_to_all | solution.py:477
  177.6 2.7 %shard_map.118.refs_0_ = bf16[512,768]{1,0:T(8,128)(2,1)S(1)} custom-call(bf16[3,256,768]{2,1,0:T(8,128)(2,1)S(1)} %copy-done.11, bf16[3,256,512]{2,1,0:T(8,128)(2,1)S(1)} %copy-done.28, bf16[3,256,768]{2,1,0:T(8,128)(2,1)S(1)} %copy-done.11, bf16[3,256,256]{2,1,0:T(8,128)(2,1)} %collective-permute-done.37.theirs_grad_ref), custom_call_target="tpu_custom_call" | custom-call | bytes 1000000 | tf_op jit(solution)/shard_map/pallas_call | solution.py:180
  180.3 6.9 %shard_map.120 = (bf16[224,2048]{1,0:T(8,128)(2,1)}, bf16[224,2048]{1,0:T(8,128)(2,1)}) custom-call(bf16[512,768]{1,0:T(8,128)(2,1)S(1)} %shard_map.118.refs_0_, bf16[512,768]{1,0:T(8,128)(2,1)S(1)} %shard_map.119.refs_1_, bf16[512,2048]{1,0:T(8,128)(2,1)} %collective-permute-done.21.refs_0_.refs_3_.refs_2_, ...), custom_call_target="tpu_custom_call" | custom-call | bytes 1000000 | tf_op jit(solution)/shard_map/pallas_call | solution.py:240
  187.3 3.2 %collective-permute-done.36 = bf16[96,2048]{1,0:T(8,128)(2,1)} collective-permute-done((bf16[96,2048]{1,0:T(8,128)(2,1)}, bf16[96,2048]{1,0:T(8,128)(2,1)}, u32[]{:S(2)}, u32[]{:S(2)}) %collective-permute-start.36) | collective-permute-done | bytes 393248 | tf_op jit(solution)/shard_map/ppermute | solution.py:49
  190.5 2.3 %add_convert_fusion = (bf16[48,2048]{1,0:T(8,128)(2,1)}, bf16[48,2048]{1,0:T(8,128)(2,1)}) fusion(bf16[96,2048]{1,0:T(8,128)(2,1)} %collective-permute-done.36, bf16[96,2048]{1,0:T(8,128)(2,1)} %collective-permute-done.35, bf16[96,2048]{1,0:T(8,128)(2,1)} %collective-permute-done.34, bf16[96,2048]{1,0:T(8,128)(2,1)S(1)} %copy-done.32), kind=kLoop, calls=%fused_computation.7 | loop fusion | flops 1572864 | bytes 1966080 | tf_op jit(solution)/shard_map/convert_element_type | solution.py:355
  192.8 2.2 %copy.11 = bf16[3584,128]{1,0:T(8,128)(2,1)} copy(bf16[3584,128]{1,0:T(8,128)(2,1)} %bitcast.3) | data formatting | bytes 1835008
  (162 shorter events, 50.3 us)
Async XLA Ops:
  2.5 25.7 %collective-permute-start = (bf16[96,2048]{1,0:T(8,128)(2,1)S(1)}, bf16[96,2048]{1,0:T(8,128)(2,1)S(1)}, u32[]{:S(2)}, u32[]{:S(2)}) collective-permute-start(bf16[96,2048]{1,0:T(8,128)(2,1)S(1)} %get-tuple-element.69.refs_1_), channel_id=1, source_target_pairs={{0,16},{16,32},{32,48},{48,0},{1,17},{17,33},{33,49},{49,1},{2,18}... | collective-permute-start | bytes 1179656 | tf_op jit(solution)/shard_map/ppermute | solution.py:49
  4.6 23.6 %collective-permute-start.1 = (bf16[96,2048]{1,0:T(8,128)(2,1)S(1)}, bf16[96,2048]{1,0:T(8,128)(2,1)S(1)}, u32[]{:S(2)}, u32[]{:S(2)}) collective-permute-start(bf16[96,2048]{1,0:T(8,128)(2,1)S(1)} %get-tuple-element.69.refs_1_), channel_id=1, source_target_pairs={{0,32},{16,48},{32,0},{48,16},{1,33},{17,49},{33,1},{49,17},{2,34}... | collective-permute-start | bytes 1179656 | tf_op jit(solution)/shard_map/ppermute | solution.py:49
  7.1 21.2 %collective-permute-start.2 = (bf16[96,2048]{1,0:T(8,128)(2,1)S(1)}, bf16[96,2048]{1,0:T(8,128)(2,1)S(1)}, u32[]{:S(2)}, u32[]{:S(2)}) collective-permute-start(bf16[96,2048]{1,0:T(8,128)(2,1)S(1)} %get-tuple-element.69.refs_1_), channel_id=1, source_target_pairs={{0,48},{16,0},{32,16},{48,32},{1,49},{17,1},{33,17},{49,33},{2,50}... | collective-permute-start | bytes 1179656 | tf_op jit(solution)/shard_map/ppermute | solution.py:49
  8.3 9.4 %collective-permute-start.8 = (bf16[32,2048]{1,0:T(8,128)(2,1)S(1)}, bf16[32,2048]{1,0:T(8,128)(2,1)S(1)}, u32[]{:S(2)}, u32[]{:S(2)}) collective-permute-start(bf16[32,2048]{1,0:T(8,128)(2,1)S(1)} %get-tuple-element.74.refs_1_), channel_id=1, source_target_pairs={{0,1},{1,2},{2,3},{3,0},{4,5},{5,6},{6,7},{7,4},{8,9},{9,10},{10,1... | collective-permute-start | bytes 393224 | tf_op jit(solution)/shard_map/ppermute | solution.py:44
  11.0 7.2 %collective-permute-start.4 = (bf16[32,2048]{1,0:T(8,128)(2,1)S(1)}, bf16[32,2048]{1,0:T(8,128)(2,1)S(1)}, u32[]{:S(2)}, u32[]{:S(2)}) collective-permute-start(bf16[32,2048]{1,0:T(8,128)(2,1)S(1)} %get-tuple-element.73.refs_1_), channel_id=1, source_target_pairs={{0,4},{1,5},{2,6},{3,7},{4,8},{5,9},{6,10},{7,11},{8,12},{9,13},{1... | collective-permute-start | bytes 393224 | tf_op jit(solution)/shard_map/ppermute | solution.py:44
  27.9 13.7 %collective-permute-start.11 = (bf16[128,2048]{1,0:T(8,128)(2,1)S(1)}, bf16[128,2048]{1,0:T(8,128)(2,1)S(1)}, u32[]{:S(2)}, u32[]{:S(2)}) collective-permute-start(bf16[128,2048]{1,0:T(8,128)(2,1)S(1)} %shard_map.95.refs_1_), channel_id=1, source_target_pairs={{0,4},{1,5},{2,6},{3,7},{4,8},{5,9},{6,10},{7,11},{8,12},{9,13},{1... | collective-permute-start | bytes 1572872 | tf_op jit(solution)/shard_map/ppermute | solution.py:44
  28.2 13.5 %collective-permute-start.7 = (bf16[128,2048]{1,0:T(8,128)(2,1)S(1)}, bf16[128,2048]{1,0:T(8,128)(2,1)S(1)}, u32[]{:S(2)}, u32[]{:S(2)}) collective-permute-start(bf16[128,2048]{1,0:T(8,128)(2,1)S(1)} %shard_map.94.refs_1_), channel_id=1, source_target_pairs={{0,16},{16,32},{32,48},{48,0},{64,112},{80,64},{96,80},{112,96},{1... | collective-permute-start | bytes 1572872 | tf_op jit(solution)/shard_map/ppermute | solution.py:44
  28.4 13.2 %collective-permute-start.3 = (bf16[128,2048]{1,0:T(8,128)(2,1)S(1)}, bf16[128,2048]{1,0:T(8,128)(2,1)S(1)}, u32[]{:S(2)}, u32[]{:S(2)}) collective-permute-start(bf16[128,2048]{1,0:T(8,128)(2,1)S(1)} %get-tuple-element.82.refs_1_), channel_id=1, source_target_pairs={{0,1},{1,2},{2,3},{3,0},{4,5},{5,6},{6,7},{7,4},{8,9},{9,10},{10,1... | collective-permute-start | bytes 1572872 | tf_op jit(solution)/shard_map/ppermute | solution.py:44
  39.6 19.9 %collective-permute-start.16 = (bf16[192,3584]{1,0:T(8,128)(2,1)S(1)}, bf16[192,3584]{1,0:T(8,128)(2,1)S(1)}, u32[]{:S(2)}, u32[]{:S(2)}) collective-permute-start(bf16[192,3584]{1,0:T(8,128)(2,1)S(1)} %convolution_convert_fusion.1.refs_0_), channel_id=1, source_target_pairs={{0,64},{64,0},{1,65},{65,1},{2,66},{66,2},{3,67},{67,3},{4,68},{68... | collective-permute-start | bytes 4128776 | tf_op jit(solution)/shard_map/ppermute | solution.py:53
  41.7 13.8 %collective-permute-start.12 = (bf16[128,2048]{1,0:T(8,128)(2,1)S(1)}, bf16[128,2048]{1,0:T(8,128)(2,1)S(1)}, u32[]{:S(2)}, u32[]{:S(2)}) collective-permute-start(bf16[128,2048]{1,0:T(8,128)(2,1)S(1)} %collective-permute-done.3.refs_2_), channel_id=1, source_target_pairs={{0,1},{1,2},{2,3},{3,0},{4,5},{5,6},{6,7},{7,4},{8,9},{9,10},{10,1... | collective-permute-start | bytes 1572872 | tf_op jit(solution)/shard_map/ppermute | solution.py:44
  43.1 12.4 %collective-permute-start.13 = (bf16[128,2048]{1,0:T(8,128)(2,1)S(1)}, bf16[128,2048]{1,0:T(8,128)(2,1)S(1)}, u32[]{:S(2)}, u32[]{:S(2)}) collective-permute-start(bf16[128,2048]{1,0:T(8,128)(2,1)S(1)} %collective-permute-done.7.refs_2_), channel_id=1, source_target_pairs={{0,16},{16,32},{32,48},{48,0},{64,112},{80,64},{96,80},{112,96},{1... | collective-permute-start | bytes 1572872 | tf_op jit(solution)/shard_map/ppermute | solution.py:44
  45.5 10.0 %collective-permute-start.14 = (bf16[128,2048]{1,0:T(8,128)(2,1)S(1)}, bf16[128,2048]{1,0:T(8,128)(2,1)S(1)}, u32[]{:S(2)}, u32[]{:S(2)}) collective-permute-start(bf16[128,2048]{1,0:T(8,128)(2,1)S(1)} %collective-permute-done.11.refs_2_), channel_id=1, source_target_pairs={{0,4},{1,5},{2,6},{3,7},{4,8},{5,9},{6,10},{7,11},{8,12},{9,13},{1... | collective-permute-start | bytes 1572872 | tf_op jit(solution)/shard_map/ppermute | solution.py:44
  55.2 13.9 %collective-permute-start.17 = (bf16[192,3584]{1,0:T(8,128)(2,1)S(1)}, bf16[192,3584]{1,0:T(8,128)(2,1)S(1)}, u32[]{:S(2)}, u32[]{:S(2)}) collective-permute-start(bf16[192,3584]{1,0:T(8,128)(2,1)S(1)} %convolution_convert_fusion.refs_2_), channel_id=1, source_target_pairs={{0,64},{64,0},{1,65},{65,1},{2,66},{66,2},{3,67},{67,3},{4,68},{68... | collective-permute-start | bytes 4128776 | tf_op jit(solution)/shard_map/ppermute | solution.py:53
  55.5 10.2 %collective-permute-start.19 = (bf16[128,2048]{1,0:T(8,128)(2,1)S(1)}, bf16[128,2048]{1,0:T(8,128)(2,1)S(1)}, u32[]{:S(2)}, u32[]{:S(2)}) collective-permute-start(bf16[128,2048]{1,0:T(8,128)(2,1)S(1)} %collective-permute-done.14.refs_3_), channel_id=1, source_target_pairs={{0,4},{1,5},{2,6},{3,7},{4,8},{5,9},{6,10},{7,11},{8,12},{9,13},{1... | collective-permute-start | bytes 1572872 | tf_op jit(solution)/shard_map/ppermute | solution.py:44
  57.3 8.4 %collective-permute-start.18 = (bf16[128,2048]{1,0:T(8,128)(2,1)S(1)}, bf16[128,2048]{1,0:T(8,128)(2,1)S(1)}, u32[]{:S(2)}, u32[]{:S(2)}) collective-permute-start(bf16[128,2048]{1,0:T(8,128)(2,1)S(1)} %collective-permute-done.13.refs_3_), channel_id=1, source_target_pairs={{0,16},{16,32},{32,48},{48,0},{64,112},{80,64},{96,80},{112,96},{1... | collective-permute-start | bytes 1572872 | tf_op jit(solution)/shard_map/ppermute | solution.py:44
  57.5 11.6 %collective-permute-start.15 = (bf16[128,2048]{1,0:T(8,128)(2,1)S(1)}, bf16[128,2048]{1,0:T(8,128)(2,1)S(1)}, u32[]{:S(2)}, u32[]{:S(2)}) collective-permute-start(bf16[128,2048]{1,0:T(8,128)(2,1)S(1)} %collective-permute-done.12.refs_3_), channel_id=1, source_target_pairs={{0,1},{1,2},{2,3},{3,0},{4,5},{5,6},{6,7},{7,4},{8,9},{9,10},{10,1... | collective-permute-start | bytes 1572872 | tf_op jit(solution)/shard_map/ppermute | solution.py:44
  65.9 27.2 %collective-permute-start.23 = (bf16[512,2048]{1,0:T(8,128)(2,1)S(1)}, bf16[512,2048]{1,0:T(8,128)(2,1)S(1)}, u32[]{:S(2)}, u32[]{:S(2)}) collective-permute-start(bf16[512,2048]{1,0:T(8,128)(2,1)S(1)} %shard_map.99.refs_2_.refs_5_.refs_4_), channel_id=1, source_target_pairs={{0,16},{16,32},{32,48},{48,0},{64,112},{80,64},{96,80},{112,96},{1... | collective-permute-start | bytes 6291464 | tf_op jit(solution)/shard_map/ppermute | solution.py:44
  67.4 28.0 %collective-permute-start.22 = (bf16[512,2048]{1,0:T(8,128)(2,1)S(1)}, bf16[512,2048]{1,0:T(8,128)(2,1)}, u32[]{:S(2)}, u32[]{:S(2)}) collective-permute-start(bf16[512,2048]{1,0:T(8,128)(2,1)S(1)} %shard_map.98.refs_1_.refs_4_.refs_3_), channel_id=1, source_target_pairs={{0,1},{1,2},{2,3},{3,0},{4,5},{5,6},{6,7},{7,4},{8,9},{9,10},{10,1... | collective-permute-start | bytes 6291464 | tf_op jit(solution)/shard_map/ppermute | solution.py:44
  70.2 28.2 %collective-permute-start.21 = (bf16[512,2048]{1,0:T(8,128)(2,1)S(1)}, bf16[512,2048]{1,0:T(8,128)(2,1)}, u32[]{:S(2)}, u32[]{:S(2)}) collective-permute-start(bf16[512,2048]{1,0:T(8,128)(2,1)S(1)} %shard_map.97.refs_0_.refs_3_.refs_2_), channel_id=1, source_target_pairs={{0,4},{1,5},{2,6},{3,7},{4,8},{5,9},{6,10},{7,11},{8,12},{9,13},{1... | collective-permute-start | bytes 6291464 | tf_op jit(solution)/shard_map/ppermute | solution.py:44
  70.5 14.7 %collective-permute-start.20 = (bf16[192,3584]{1,0:T(8,128)(2,1)}, bf16[192,3584]{1,0:T(8,128)(2,1)}, u32[]{:S(2)}, u32[]{:S(2)}) collective-permute-start(bf16[192,3584]{1,0:T(8,128)(2,1)} %shard_map.96.refs_4_), channel_id=1, source_target_pairs={{0,64},{64,0},{1,65},{65,1},{2,66},{66,2},{3,67},{67,3},{4,68},{68... | collective-permute-start | bytes 4128776 | tf_op jit(solution)/shard_map/ppermute | solution.py:53
  93.1 32.5 %collective-permute-start.30 = (bf16[512,2048]{1,0:T(8,128)(2,1)S(1)}, bf16[512,2048]{1,0:T(8,128)(2,1)}, u32[]{:S(2)}, u32[]{:S(2)}) collective-permute-start(bf16[512,2048]{1,0:T(8,128)(2,1)S(1)} %collective-permute-done.23.refs_2_.refs_5_.refs_4_), channel_id=1, source_target_pairs={{0,16},{16,32},{32,48},{48,0},{64,112},{80,64},{96,80},{112,96},{1... | collective-permute-start | bytes 6291464 | tf_op jit(solution)/shard_map/ppermute | solution.py:44
  95.4 30.3 %collective-permute-start.28 = (bf16[512,2048]{1,0:T(8,128)(2,1)}, bf16[512,2048]{1,0:T(8,128)(2,1)}, u32[]{:S(2)}, u32[]{:S(2)}) collective-permute-start(bf16[512,2048]{1,0:T(8,128)(2,1)} %collective-permute-done.22.refs_1_.refs_4_.refs_3_), channel_id=1, source_target_pairs={{0,1},{1,2},{2,3},{3,0},{4,5},{5,6},{6,7},{7,4},{8,9},{9,10},{10,1... | collective-permute-start | bytes 6291464 | tf_op jit(solution)/shard_map/ppermute | solution.py:44
  98.4 29.5 %collective-permute-start.24 = (bf16[512,2048]{1,0:T(8,128)(2,1)}, bf16[512,2048]{1,0:T(8,128)(2,1)}, u32[]{:S(2)}, u32[]{:S(2)}) collective-permute-start(bf16[512,2048]{1,0:T(8,128)(2,1)} %collective-permute-done.21.refs_0_.refs_3_.refs_2_), channel_id=1, source_target_pairs={{0,4},{1,5},{2,6},{3,7},{4,8},{5,9},{6,10},{7,11},{8,12},{9,13},{1... | collective-permute-start | bytes 6291464 | tf_op jit(solution)/shard_map/ppermute | solution.py:44
  99.7 24.3 %collective-permute-start.25 = (bf16[3,256,768]{2,1,0:T(8,128)(2,1)}, bf16[3,256,768]{2,1,0:T(8,128)(2,1)}, u32[]{:S(2)}, u32[]{:S(2)}) collective-permute-start(bf16[3,256,768]{2,1,0:T(8,128)(2,1)} %shard_map.101.mine_ref.mine_grad_ref), channel_id=1, source_target_pairs={{0,64},{64,0},{1,65},{65,1},{2,66},{66,2},{3,67},{67,3},{4,68},{68... | collective-permute-start | bytes 3538952 | tf_op jit(solution)/shard_map/ppermute | solution.py:53
  125.7 28.4 %collective-permute-start.31 = (bf16[512,2048]{1,0:T(8,128)(2,1)}, bf16[512,2048]{1,0:T(8,128)(2,1)S(1)}, u32[]{:S(2)}, u32[]{:S(2)}) collective-permute-start(bf16[512,2048]{1,0:T(8,128)(2,1)} %collective-permute-done.30.refs_2_.refs_5_.refs_7_), channel_id=1, source_target_pairs={{0,16},{16,32},{32,48},{48,0},{64,112},{80,64},{96,80},{112,96},{1... | collective-permute-start | bytes 6291464 | tf_op jit(solution)/shard_map/ppermute | solution.py:44
  125.8 28.3 %collective-permute-start.29 = (bf16[512,2048]{1,0:T(8,128)(2,1)}, bf16[512,2048]{1,0:T(8,128)(2,1)S(1)}, u32[]{:S(2)}, u32[]{:S(2)}) collective-permute-start(bf16[512,2048]{1,0:T(8,128)(2,1)} %collective-permute-done.28.refs_1_.refs_4_.refs_6_), channel_id=1, source_target_pairs={{0,1},{1,2},{2,3},{3,0},{4,5},{5,6},{6,7},{7,4},{8,9},{9,10},{10,1... | collective-permute-start | bytes 6291464 | tf_op jit(solution)/shard_map/ppermute | solution.py:44
  127.8 26.2 %collective-permute-start.27 = (bf16[512,2048]{1,0:T(8,128)(2,1)}, bf16[512,2048]{1,0:T(8,128)(2,1)}, u32[]{:S(2)}, u32[]{:S(2)}) collective-permute-start(bf16[512,2048]{1,0:T(8,128)(2,1)} %collective-permute-done.24.refs_0_.refs_3_.refs_5_), channel_id=1, source_target_pairs={{0,4},{1,5},{2,6},{3,7},{4,8},{5,9},{6,10},{7,11},{8,12},{9,13},{1... | collective-permute-start | bytes 6291464 | tf_op jit(solution)/shard_map/ppermute | solution.py:44
  161.4 15.6 %collective-permute-start.37 = (bf16[3,256,256]{2,1,0:T(8,128)(2,1)S(1)}, bf16[3,256,256]{2,1,0:T(8,128)(2,1)}, u32[]{:S(2)}, u32[]{:S(2)}) collective-permute-start(bf16[3,256,256]{2,1,0:T(8,128)(2,1)S(1)} %shard_map.117.mine_grad_ref), channel_id=1, source_target_pairs={{0,64},{64,0},{1,65},{65,1},{2,66},{66,2},{3,67},{67,3},{4,68},{68... | collective-permute-start | bytes 1179656 | tf_op jit(solution)/shard_map/ppermute | solution.py:53
  167.6 19.6 %collective-permute-start.34 = (bf16[96,2048]{1,0:T(8,128)(2,1)}, bf16[96,2048]{1,0:T(8,128)(2,1)}, u32[]{:S(2)}, u32[]{:S(2)}) collective-permute-start(bf16[96,2048]{1,0:T(8,128)(2,1)} %get-tuple-element.123), channel_id=1, source_target_pairs={{0,48},{16,0},{32,16},{48,32},{1,49},{17,1},{33,17},{49,33},{2,50}... | collective-permute-start | bytes 1179656 | tf_op jit(solution)/shard_map/ppermute | solution.py:49
  169.8 17.4 %collective-permute-start.35 = (bf16[96,2048]{1,0:T(8,128)(2,1)}, bf16[96,2048]{1,0:T(8,128)(2,1)}, u32[]{:S(2)}, u32[]{:S(2)}) collective-permute-start(bf16[96,2048]{1,0:T(8,128)(2,1)} %get-tuple-element.124), channel_id=1, source_target_pairs={{0,32},{16,48},{32,0},{48,16},{1,33},{17,49},{33,1},{49,17},{2,34}... | collective-permute-start | bytes 1179656 | tf_op jit(solution)/shard_map/ppermute | solution.py:49
  169.8 20.7 %collective-permute-start.36 = (bf16[96,2048]{1,0:T(8,128)(2,1)}, bf16[96,2048]{1,0:T(8,128)(2,1)}, u32[]{:S(2)}, u32[]{:S(2)}) collective-permute-start(bf16[96,2048]{1,0:T(8,128)(2,1)} %get-tuple-element.125), channel_id=1, source_target_pairs={{0,16},{16,32},{32,48},{48,0},{1,17},{17,33},{33,49},{49,1},{2,18}... | collective-permute-start | bytes 1179656 | tf_op jit(solution)/shard_map/ppermute | solution.py:49
  170.5 22.3 %all-to-all-start = ((bf16[16,224,128]{2,1,0:T(8,128)(2,1)}), bf16[16,224,128]{2,1,0:T(8,128)(2,1)}, u32[]{:S(2)}, u32[]{:S(2)}) async-start(bf16[16,224,128]{2,1,0:T(8,128)(2,1)} %copy-done.26), calls=%async_computation | async-start | bytes 1835008 | tf_op jit(solution)/shard_map/all_to_all | solution.py:477
  (46 other events, 280.6 us)

commit v2 on v1

--- a/solution.py
+++ b/solution.py
@@ -430,7 +430,7 @@
     (gate_part_,) = tie((gate_part,), u0)
     grads = slice_grads((gate_part_, *gate_up, grad_part, grad_theirs))
 
-    both.append(hops(both[1], *grads))
+    both.append(hops(both[1], *grads, v0))
     toks.append([(x, 0) for x in both[1]])
     cots.append([(x, 1) for x in both[1]])
     input_part = input_product(tie(tuple(grads), *both[1]), gate_weight, up_weight)

time: 196 us -> 196 us (level)
  Pallas kernels: 93.8 us -> 88.9 us
  waiting for transfers between devices: 5.41 us -> 8.74 us
    pallas_call x8, Pallas kernels: 11.9 us -> 8.44 us  [activations(): pl.pallas_call(kernel, grid=(n_parts,), in_specs=[spec(columns, block) fo...]
    unnamed x79 -> x91, local copies, waits for them, and re-layouts: 14.1 us -> 15.2 us
  transfers between devices with their start and end apart: 39 -> 39, of which waited for: 3 -> 7; matrix products, arithmetic and copies ran while one was open for 13% -> 13% of each run, Pallas kernels for 46% -> 44%
where the time goes in v2:
time: 196 us; the launch traced here: 195 us
  Pallas kernels  88.9 us (45%)
  starting transfers between devices  56.5 us (29%)
  local copies, waits for them, and re-layouts  20.6 us (11%)
  matrix products  16.5 us (8%)
  waiting for transfers between devices  8.74 us (4%)
  other arithmetic  2.65 us (1%)
    ppermute x24, starting transfers between devices, hop(): return lax.ppermute(array, ('row', mesh_axis(axis)), pairs)  38.1 us
    pallas_call x4, Pallas kernels, weight_grad(): pl.pallas_call(lambda *refs: weight_grad_kernel(n_groups, n_parts, before...  23.3 us
    pallas_call x5, Pallas kernels, own_partials(): pl.pallas_call(lambda *refs: own_partials_kernel(n_parts, sides, *refs),...  17.5 us
    dot_general x2, matrix products, plain(): return jnp.dot(left, right, preferred_element_type=F32)  16.5 us
    pallas_call x1, Pallas kernels, input_product(): pl.pallas_call(input_kernel, grid=(features // block,), in_specs=[*map(wh...  16.2 us
    unnamed x91, local copies, waits for them, and re-layouts  15.2 us
    pallas_call x1, Pallas kernels, mixed_product(): pl.pallas_call(mixed_kernel, grid=(features // block,), in_specs=[*map(wh...  9.86 us
    ppermute x6, starting transfers between devices, shift(): return lax.ppermute(array, mesh_axis(axis), pairs)  9.32 us
  transfers between devices with their start and end apart: 39, of which 7 were waited for; matrix products, arithmetic and copies ran while one was open for 13% of the time, Pallas kernels for 44%

profile of v2, /device:TPU:1, one launch (start us, length us, event | category | flops | bytes accessed | tf_op | source)
XLA Modules:
  0.0 195.2 jit_solution(14704921031151213381)
XLA Ops:
  2.5 2.1 %collective-permute-start = (bf16[96,2048]{1,0:T(8,128)(2,1)S(1)}, bf16[96,2048]{1,0:T(8,128)(2,1)S(1)}, u32[]{:S(2)}, u32[]{:S(2)}) collective-permute-start(bf16[96,2048]{1,0:T(8,128)(2,1)S(1)} %get-tuple-element.69.refs_1_), channel_id=1, source_target_pairs={{0,16},{16,32},{32,48},{48,0},{1,17},{17,33},{33,49},{49,1},{2,18}... | collective-permute-start | bytes 1179656 | tf_op jit(solution)/shard_map/ppermute | solution.py:49
  4.6 2.5 %collective-permute-start.1 = (bf16[96,2048]{1,0:T(8,128)(2,1)S(1)}, bf16[96,2048]{1,0:T(8,128)(2,1)S(1)}, u32[]{:S(2)}, u32[]{:S(2)}) collective-permute-start(bf16[96,2048]{1,0:T(8,128)(2,1)S(1)} %get-tuple-element.69.refs_1_), channel_id=1, source_target_pairs={{0,32},{16,48},{32,0},{48,16},{1,33},{17,49},{33,1},{49,17},{2,34}... | collective-permute-start | bytes 1179656 | tf_op jit(solution)/shard_map/ppermute | solution.py:49
  8.3 2.7 %collective-permute-start.8 = (bf16[32,2048]{1,0:T(8,128)(2,1)S(1)}, bf16[32,2048]{1,0:T(8,128)(2,1)S(1)}, u32[]{:S(2)}, u32[]{:S(2)}) collective-permute-start(bf16[32,2048]{1,0:T(8,128)(2,1)S(1)} %get-tuple-element.74.refs_1_), channel_id=1, source_target_pairs={{0,1},{1,2},{2,3},{3,0},{4,5},{5,6},{6,7},{7,4},{8,9},{9,10},{10,1... | collective-permute-start | bytes 393224 | tf_op jit(solution)/shard_map/ppermute | solution.py:44
  11.0 3.8 %collective-permute-start.4 = (bf16[32,2048]{1,0:T(8,128)(2,1)S(1)}, bf16[32,2048]{1,0:T(8,128)(2,1)S(1)}, u32[]{:S(2)}, u32[]{:S(2)}) collective-permute-start(bf16[32,2048]{1,0:T(8,128)(2,1)S(1)} %get-tuple-element.73.refs_1_), channel_id=1, source_target_pairs={{0,4},{1,5},{2,6},{3,7},{4,8},{5,9},{6,10},{7,11},{8,12},{9,13},{1... | collective-permute-start | bytes 393224 | tf_op jit(solution)/shard_map/ppermute | solution.py:44
  14.7 2.9 %constant_dynamic-slice_fusion.1 = (bf16[2048,224]{1,0:T(8,128)(2,1)S(1)}, bf16[2048,224]{1,0:T(8,128)(2,1)S(1)}) fusion(bf16[2048,3584]{1,0:T(8,128)(2,1)} %up_ref.1, s32[]{:T(128)S(6)} %select_n.2, bf16[2048,3584]{1,0:T(8,128)(2,1)} %gate_ref.1), kind=kLoop, calls=%fused_computation.10 | loop fusion | bytes 3670020 | tf_op jit(solution)/shard_map/dynamic_slice | solution.py:389
  28.4 2.8 %collective-permute-start.3 = (bf16[128,2048]{1,0:T(8,128)(2,1)S(1)}, bf16[128,2048]{1,0:T(8,128)(2,1)S(1)}, u32[]{:S(2)}, u32[]{:S(2)}) collective-permute-start(bf16[128,2048]{1,0:T(8,128)(2,1)S(1)} %get-tuple-element.82.refs_1_), channel_id=1, source_target_pairs={{0,1},{1,2},{2,3},{3,0},{4,5},{5,6},{6,7},{7,4},{8,9},{9,10},{10,1... | collective-permute-start | bytes 1572872 | tf_op jit(solution)/shard_map/ppermute | solution.py:44
  31.2 8.3 %convolution_convert_fusion.1.refs_0_ = bf16[192,3584]{1,0:T(8,128)(2,1)S(1)} fusion(bf16[192,2048]{1,0:T(8,128)(2,1)S(1)} %get-tuple-element.78, bf16[2048,3584]{1,0:T(8,128)(2,1)} %gate_ref.1), kind=kOutput, calls=%fused_computation.1 | convolution fusion | flops 2819260416 | bytes 16842752 | tf_op jit(solution)/shard_map/dot_general | solution.py:100
  39.6 2.1 %collective-permute-start.16 = (bf16[192,3584]{1,0:T(8,128)(2,1)S(1)}, bf16[192,3584]{1,0:T(8,128)(2,1)S(1)}, u32[]{:S(2)}, u32[]{:S(2)}) collective-permute-start(bf16[192,3584]{1,0:T(8,128)(2,1)S(1)} %convolution_convert_fusion.1.refs_0_), channel_id=1, source_target_pairs={{0,64},{64,0},{1,65},{65,1},{2,66},{66,2},{3,67},{67,3},{4,68},{68... | collective-permute-start | bytes 4128776 | tf_op jit(solution)/shard_map/ppermute | solution.py:53
  43.1 2.4 %collective-permute-start.13 = (bf16[128,2048]{1,0:T(8,128)(2,1)S(1)}, bf16[128,2048]{1,0:T(8,128)(2,1)S(1)}, u32[]{:S(2)}, u32[]{:S(2)}) collective-permute-start(bf16[128,2048]{1,0:T(8,128)(2,1)S(1)} %collective-permute-done.7.refs_2_), channel_id=1, source_target_pairs={{0,16},{16,32},{32,48},{48,0},{64,112},{80,64},{96,80},{112,96},{1... | collective-permute-start | bytes 1572872 | tf_op jit(solution)/shard_map/ppermute | solution.py:44
  47.0 8.2 %convolution_convert_fusion.refs_2_ = bf16[192,3584]{1,0:T(8,128)(2,1)S(1)} fusion(bf16[192,2048]{1,0:T(8,128)(2,1)S(1)} %get-tuple-element.78, bf16[2048,3584]{1,0:T(8,128)(2,1)} %up_ref.1), kind=kOutput, calls=%fused_computation | convolution fusion | flops 2819260416 | bytes 16842752 | tf_op jit(solution)/shard_map/dot_general | solution.py:100
  59.5 6.2 %shard_map.96.refs_4_ = bf16[192,3584]{1,0:T(8,128)(2,1)} custom-call(bf16[192,2048]{1,0:T(8,128)(2,1)S(1)} %get-tuple-element.81.left_ref, bf16[3584,2048]{1,0:T(8,128)(2,1)S(1)} %bitcast.9), custom_call_target="tpu_custom_call" | custom-call | flops 11274289152 | bytes 58720256 | tf_op jit(solution)/shard_map/pallas_call | solution.py:258
  70.5 9.9 %shard_map.100.refs_1_ = bf16[192,2048]{1,0:T(8,128)(2,1)S(1)} custom-call(bf16[192,3584]{1,0:T(8,128)(2,1)} %copy-done.22, bf16[192,3584]{1,0:T(8,128)(2,1)} %copy-done.24, bf16[192,3584]{1,0:T(8,128)(2,1)} %copy-done.26, bf16[192,3584]{1,0:T(8,128)(2,1)} %copy-done.28, bf16[3584,2048]{1,0:T(8,128)(2,1)} %refs_4_.1), custom_call_target="tpu_custom_call" | custom-call | bytes 1000000 | tf_op jit(solution)/shard_map/pallas_call | solution.py:300
  81.6 2.9 %shard_map.101.mine_ref.mine_grad_ref = bf16[3,256,768]{2,1,0:T(8,128)(2,1)S(1)} custom-call(bf16[512,2048]{1,0:T(8,128)(2,1)S(1)} %shard_map.97.refs_0_.refs_3_.refs_2_, bf16[512,2048]{1,0:T(8,128)(2,1)S(1)} %shard_map.98.refs_1_.refs_4_.refs_3_, bf16[512,2048]{1,0:T(8,128)(2,1)S(1)} %shard_map.99.refs_2_.refs_5_.refs_4_, ...), custom_call_target="tpu_custom_call" | custom-call | bytes 1000000 | tf_op jit(solution)/shard_map/pallas_call | solution.py:137
  85.1 5.6 %shard_map.102 = (bf16[192,3584]{1,0:T(8,128)(2,1)S(1)}, bf16[192,3584]{1,0:T(8,128)(2,1)S(1)}) custom-call(bf16[192,3584]{1,0:T(8,128)(2,1)S(1)} %copy-done.23, bf16[192,3584]{1,0:T(8,128)(2,1)S(1)} %copy-done.25, bf16[192,3584]{1,0:T(8,128)(2,1)S(1)} %copy-done.27, bf16[192,3584]{1,0:T(8,128)(2,1)S(1)} %copy-done.29, bf16[192,3584]{1,0:T(8,128)(2,1)} %shard_map.96.refs_4_, ...), custom_call_target="tpu_custom_call" | custom-call | bytes 1000000 | tf_op jit(solution)/shard_map/pallas_call | solution.py:319
  94.0 2.0 %collective-permute-start.30 = (bf16[512,2048]{1,0:T(8,128)(2,1)S(1)}, bf16[512,2048]{1,0:T(8,128)(2,1)}, u32[]{:S(2)}, u32[]{:S(2)}) collective-permute-start(bf16[512,2048]{1,0:T(8,128)(2,1)S(1)} %collective-permute-done.23.refs_2_.refs_5_.refs_4_), channel_id=1, source_target_pairs={{0,16},{16,32},{32,48},{48,0},{64,112},{80,64},{96,80},{112,96},{1... | collective-permute-start | bytes 6291464 | tf_op jit(solution)/shard_map/ppermute | solution.py:44
  96.0 2.9 %collective-permute-start.28 = (bf16[512,2048]{1,0:T(8,128)(2,1)}, bf16[512,2048]{1,0:T(8,128)(2,1)}, u32[]{:S(2)}, u32[]{:S(2)}) collective-permute-start(bf16[512,2048]{1,0:T(8,128)(2,1)} %collective-permute-done.22.refs_1_.refs_4_.refs_3_), channel_id=1, source_target_pairs={{0,1},{1,2},{2,3},{3,0},{4,5},{5,6},{6,7},{7,4},{8,9},{9,10},{10,1... | collective-permute-start | bytes 6291464 | tf_op jit(solution)/shard_map/ppermute | solution.py:44
  100.3 16.2 %shard_map.103.refs_2_ = bf16[192,2048]{1,0:T(8,128)(2,1)S(1)} custom-call(bf16[192,3584]{1,0:T(8,128)(2,1)} %copy-done.35, bf16[192,3584]{1,0:T(8,128)(2,1)} %copy-done.36, bf16[2048,3584]{1,0:T(8,128)(2,1)} %gate_ref.1, bf16[2048,3584]{1,0:T(8,128)(2,1)} %up_ref.1), custom_call_target="tpu_custom_call" | custom-call | bytes 1000000 | tf_op jit(solution)/shard_map/pallas_call | solution.py:340
  117.8 4.4 %shard_map.105.mine_ref.mine_grad_ref = bf16[3,256,768]{2,1,0:T(8,128)(2,1)S(1)} custom-call(bf16[512,2048]{1,0:T(8,128)(2,1)} %collective-permute-done.21.refs_0_.refs_3_.refs_2_, bf16[512,2048]{1,0:T(8,128)(2,1)} %collective-permute-done.22.refs_1_.refs_4_.refs_3_, bf16[512,2048]{1,0:T(8,128)(2,1)S(1)} %collective-permute-done.23.refs_2_.refs_5_.refs_4_, ...), custom_call_target="tpu_custom_call" | custom-call | bytes 1000000 | tf_op jit(solution)/shard_map/pallas_call | solution.py:137
  127.5 2.5 %collective-permute-start.27 = (bf16[512,2048]{1,0:T(8,128)(2,1)}, bf16[512,2048]{1,0:T(8,128)(2,1)}, u32[]{:S(2)}, u32[]{:S(2)}) collective-permute-start(bf16[512,2048]{1,0:T(8,128)(2,1)} %collective-permute-done.25.refs_0_.refs_3_.refs_5_), channel_id=1, source_target_pairs={{0,4},{1,5},{2,6},{3,7},{4,8},{5,9},{6,10},{7,11},{8,12},{9,13},{1... | collective-permute-start | bytes 6291464 | tf_op jit(solution)/shard_map/ppermute | solution.py:44
  129.9 4.7 %shard_map.106.mine_ref.mine_grad_ref = bf16[3,256,768]{2,1,0:T(8,128)(2,1)S(1)} custom-call(bf16[512,2048]{1,0:T(8,128)(2,1)} %collective-permute-done.25.refs_0_.refs_3_.refs_5_, bf16[512,2048]{1,0:T(8,128)(2,1)} %collective-permute-done.28.refs_1_.refs_4_.refs_6_, bf16[512,2048]{1,0:T(8,128)(2,1)} %collective-permute-done.30.refs_2_.refs_5_.refs_7_, ...), custom_call_target="tpu_custom_call" | custom-call | bytes 1000000 | tf_op jit(solution)/shard_map/pallas_call | solution.py:137
  139.4 4.4 %shard_map.111.refs_8_ = f32[256,2048]{1,0:T(8,128)S(1)} custom-call(bf16[256,768]{1,0:T(8,128)(2,1)S(1)} %shard_map.109.refs_0_, bf16[256,768]{1,0:T(8,128)(2,1)S(1)} %shard_map.110.refs_1_, bf16[512,2048]{1,0:T(8,128)(2,1)S(1)} %shard_map.97.refs_0_.refs_3_.refs_2_, bf16[512,2048]{1,0:T(8,128)(2,1)S(1)} %shard_map.98.refs_1_.refs_4_.refs_3_, ...), custom_call_target="tpu_custom_call" | custom-call | bytes 1000000 | tf_op jit(solution)/shard_map/pallas_call | solution.py:240
  143.8 7.4 %shard_map.112.refs_8_ = f32[512,2048]{1,0:T(8,128)} custom-call(bf16[512,768]{1,0:T(8,128)(2,1)S(1)} %copy-done.32, bf16[512,768]{1,0:T(8,128)(2,1)S(1)} %shard_map.108.refs_1_, bf16[512,2048]{1,0:T(8,128)(2,1)S(1)} %shard_map.97.refs_0_.refs_3_.refs_2_, bf16[512,2048]{1,0:T(8,128)(2,1)S(1)} %shard_map.98.refs_1_.refs_4_.refs_3_, ...), custom_call_target="tpu_custom_call" | custom-call | bytes 1000000 | tf_op jit(solution)/shard_map/pallas_call | solution.py:240
  153.2 3.0 %shard_map.113.mine_ref = bf16[3,256,512]{2,1,0:T(8,128)(2,1)S(1)} custom-call(bf16[512,2048]{1,0:T(8,128)(2,1)} %collective-permute-done.27.refs_0_.refs_5_, bf16[512,2048]{1,0:T(8,128)(2,1)S(1)} %collective-permute-done.29.refs_1_.refs_6_, bf16[512,2048]{1,0:T(8,128)(2,1)S(1)} %collective-permute-done.31.refs_2_.refs_7_, ...), custom_call_target="tpu_custom_call" | custom-call | bytes 1000000 | tf_op jit(solution)/shard_map/pallas_call | solution.py:137
  158.4 2.5 %shard_map.117.mine_grad_ref = bf16[3,256,256]{2,1,0:T(8,128)(2,1)S(1)} custom-call(bf16[512,2048]{1,0:T(8,128)(2,1)} %collective-permute-done.27.refs_0_.refs_5_, bf16[512,2048]{1,0:T(8,128)(2,1)S(1)} %collective-permute-done.29.refs_1_.refs_6_, bf16[512,2048]{1,0:T(8,128)(2,1)S(1)} %collective-permute-done.31.refs_2_.refs_7_, bf16[256,2048]{1,0:T(8,128)(2,1)S(1)} %copy-done.8), custom_call_target="tpu_custom_call" | custom-call | bytes 1000000 | tf_op jit(solution)/shard_map/pallas_call | solution.py:137
  162.6 4.5 %shard_map.116 = bf16[16,224,128]{2,1,0:T(8,128)(2,1)S(1)} custom-call(bf16[256,768]{1,0:T(8,128)(2,1)S(1)} %shard_map.115.refs_0_, bf16[256,768]{1,0:T(8,128)(2,1)S(1)} %shard_map.114.refs_1_, bf16[512,2048]{1,0:T(8,128)(2,1)} %collective-permute-done.21.refs_0_.refs_3_.refs_2_, bf16[512,2048]{1,0:T(8,128)(2,1)} %collective-permute-done.22.refs_1_.refs_4_.refs_3_, ...), custom_call_target="tpu_custom_call" | custom-call | bytes 1000000 | tf_op jit(solution)/shard_map/pallas_call | solution.py:240
  167.2 2.9 %collective-permute-start.34 = (bf16[96,2048]{1,0:T(8,128)(2,1)}, bf16[96,2048]{1,0:T(8,128)(2,1)}, u32[]{:S(2)}, u32[]{:S(2)}) collective-permute-start(bf16[96,2048]{1,0:T(8,128)(2,1)} %get-tuple-element.123), channel_id=1, source_target_pairs={{0,48},{16,0},{32,16},{48,32},{1,49},{17,1},{33,17},{49,33},{2,50}... | collective-permute-start | bytes 1179656 | tf_op jit(solution)/shard_map/ppermute | solution.py:49
  170.8 4.3 %all-to-all-start = ((bf16[16,224,128]{2,1,0:T(8,128)(2,1)}), bf16[16,224,128]{2,1,0:T(8,128)(2,1)}, u32[]{:S(2)}, u32[]{:S(2)}) async-start(bf16[16,224,128]{2,1,0:T(8,128)(2,1)} %copy-done.30), calls=%async_computation | async-start | bytes 1835008 | tf_op jit(solution)/shard_map/all_to_all | solution.py:477
  177.8 2.7 %shard_map.118.refs_0_ = bf16[512,768]{1,0:T(8,128)(2,1)S(1)} custom-call(bf16[3,256,768]{2,1,0:T(8,128)(2,1)S(1)} %copy-done.11, bf16[3,256,512]{2,1,0:T(8,128)(2,1)S(1)} %copy-done.34, bf16[3,256,768]{2,1,0:T(8,128)(2,1)S(1)} %copy-done.11, bf16[3,256,256]{2,1,0:T(8,128)(2,1)} %collective-permute-done.37.theirs_grad_ref), custom_call_target="tpu_custom_call" | custom-call | bytes 1000000 | tf_op jit(solution)/shard_map/pallas_call | solution.py:180
  180.6 6.9 %shard_map.120 = (bf16[224,2048]{1,0:T(8,128)(2,1)}, bf16[224,2048]{1,0:T(8,128)(2,1)}) custom-call(bf16[512,768]{1,0:T(8,128)(2,1)S(1)} %shard_map.118.refs_0_, bf16[512,768]{1,0:T(8,128)(2,1)S(1)} %shard_map.119.refs_1_, bf16[512,2048]{1,0:T(8,128)(2,1)} %collective-permute-done.21.refs_0_.refs_3_.refs_2_, ...), custom_call_target="tpu_custom_call" | custom-call | bytes 1000000 | tf_op jit(solution)/shard_map/pallas_call | solution.py:240
  187.5 3.2 %collective-permute-done.36 = bf16[96,2048]{1,0:T(8,128)(2,1)} collective-permute-done((bf16[96,2048]{1,0:T(8,128)(2,1)}, bf16[96,2048]{1,0:T(8,128)(2,1)}, u32[]{:S(2)}, u32[]{:S(2)}) %collective-permute-start.36) | collective-permute-done | bytes 393248 | tf_op jit(solution)/shard_map/ppermute | solution.py:49
  190.8 2.3 %add_convert_fusion = (bf16[48,2048]{1,0:T(8,128)(2,1)}, bf16[48,2048]{1,0:T(8,128)(2,1)}) fusion(bf16[96,2048]{1,0:T(8,128)(2,1)} %collective-permute-done.36, bf16[96,2048]{1,0:T(8,128)(2,1)} %collective-permute-done.35, bf16[96,2048]{1,0:T(8,128)(2,1)} %collective-permute-done.34, bf16[96,2048]{1,0:T(8,128)(2,1)S(1)} %copy-done.38), kind=kLoop, calls=%fused_computation.7 | loop fusion | flops 1572864 | bytes 1966080 | tf_op jit(solution)/shard_map/convert_element_type | solution.py:355
  193.1 2.2 %copy.11 = bf16[3584,128]{1,0:T(8,128)(2,1)} copy(bf16[3584,128]{1,0:T(8,128)(2,1)} %bitcast.3) | data formatting | bytes 1835008
  (174 shorter events, 52.3 us)
Async XLA Ops:
  2.5 25.7 %collective-permute-start = (bf16[96,2048]{1,0:T(8,128)(2,1)S(1)}, bf16[96,2048]{1,0:T(8,128)(2,1)S(1)}, u32[]{:S(2)}, u32[]{:S(2)}) collective-permute-start(bf16[96,2048]{1,0:T(8,128)(2,1)S(1)} %get-tuple-element.69.refs_1_), channel_id=1, source_target_pairs={{0,16},{16,32},{32,48},{48,0},{1,17},{17,33},{33,49},{49,1},{2,18}... | collective-permute-start | bytes 1179656 | tf_op jit(solution)/shard_map/ppermute | solution.py:49
  4.6 23.6 %collective-permute-start.1 = (bf16[96,2048]{1,0:T(8,128)(2,1)S(1)}, bf16[96,2048]{1,0:T(8,128)(2,1)S(1)}, u32[]{:S(2)}, u32[]{:S(2)}) collective-permute-start(bf16[96,2048]{1,0:T(8,128)(2,1)S(1)} %get-tuple-element.69.refs_1_), channel_id=1, source_target_pairs={{0,32},{16,48},{32,0},{48,16},{1,33},{17,49},{33,1},{49,17},{2,34}... | collective-permute-start | bytes 1179656 | tf_op jit(solution)/shard_map/ppermute | solution.py:49
  7.1 21.1 %collective-permute-start.2 = (bf16[96,2048]{1,0:T(8,128)(2,1)S(1)}, bf16[96,2048]{1,0:T(8,128)(2,1)S(1)}, u32[]{:S(2)}, u32[]{:S(2)}) collective-permute-start(bf16[96,2048]{1,0:T(8,128)(2,1)S(1)} %get-tuple-element.69.refs_1_), channel_id=1, source_target_pairs={{0,48},{16,0},{32,16},{48,32},{1,49},{17,1},{33,17},{49,33},{2,50}... | collective-permute-start | bytes 1179656 | tf_op jit(solution)/shard_map/ppermute | solution.py:49
  8.3 9.4 %collective-permute-start.8 = (bf16[32,2048]{1,0:T(8,128)(2,1)S(1)}, bf16[32,2048]{1,0:T(8,128)(2,1)S(1)}, u32[]{:S(2)}, u32[]{:S(2)}) collective-permute-start(bf16[32,2048]{1,0:T(8,128)(2,1)S(1)} %get-tuple-element.74.refs_1_), channel_id=1, source_target_pairs={{0,1},{1,2},{2,3},{3,0},{4,5},{5,6},{6,7},{7,4},{8,9},{9,10},{10,1... | collective-permute-start | bytes 393224 | tf_op jit(solution)/shard_map/ppermute | solution.py:44
  11.0 7.2 %collective-permute-start.4 = (bf16[32,2048]{1,0:T(8,128)(2,1)S(1)}, bf16[32,2048]{1,0:T(8,128)(2,1)S(1)}, u32[]{:S(2)}, u32[]{:S(2)}) collective-permute-start(bf16[32,2048]{1,0:T(8,128)(2,1)S(1)} %get-tuple-element.73.refs_1_), channel_id=1, source_target_pairs={{0,4},{1,5},{2,6},{3,7},{4,8},{5,9},{6,10},{7,11},{8,12},{9,13},{1... | collective-permute-start | bytes 393224 | tf_op jit(solution)/shard_map/ppermute | solution.py:44
  27.9 13.8 %collective-permute-start.11 = (bf16[128,2048]{1,0:T(8,128)(2,1)S(1)}, bf16[128,2048]{1,0:T(8,128)(2,1)S(1)}, u32[]{:S(2)}, u32[]{:S(2)}) collective-permute-start(bf16[128,2048]{1,0:T(8,128)(2,1)S(1)} %shard_map.95.refs_1_), channel_id=1, source_target_pairs={{0,4},{1,5},{2,6},{3,7},{4,8},{5,9},{6,10},{7,11},{8,12},{9,13},{1... | collective-permute-start | bytes 1572872 | tf_op jit(solution)/shard_map/ppermute | solution.py:44
  28.1 13.6 %collective-permute-start.7 = (bf16[128,2048]{1,0:T(8,128)(2,1)S(1)}, bf16[128,2048]{1,0:T(8,128)(2,1)S(1)}, u32[]{:S(2)}, u32[]{:S(2)}) collective-permute-start(bf16[128,2048]{1,0:T(8,128)(2,1)S(1)} %shard_map.94.refs_1_), channel_id=1, source_target_pairs={{0,16},{16,32},{32,48},{48,0},{64,112},{80,64},{96,80},{112,96},{1... | collective-permute-start | bytes 1572872 | tf_op jit(solution)/shard_map/ppermute | solution.py:44
  28.4 13.3 %collective-permute-start.3 = (bf16[128,2048]{1,0:T(8,128)(2,1)S(1)}, bf16[128,2048]{1,0:T(8,128)(2,1)S(1)}, u32[]{:S(2)}, u32[]{:S(2)}) collective-permute-start(bf16[128,2048]{1,0:T(8,128)(2,1)S(1)} %get-tuple-element.82.refs_1_), channel_id=1, source_target_pairs={{0,1},{1,2},{2,3},{3,0},{4,5},{5,6},{6,7},{7,4},{8,9},{9,10},{10,1... | collective-permute-start | bytes 1572872 | tf_op jit(solution)/shard_map/ppermute | solution.py:44
  39.6 19.9 %collective-permute-start.16 = (bf16[192,3584]{1,0:T(8,128)(2,1)S(1)}, bf16[192,3584]{1,0:T(8,128)(2,1)S(1)}, u32[]{:S(2)}, u32[]{:S(2)}) collective-permute-start(bf16[192,3584]{1,0:T(8,128)(2,1)S(1)} %convolution_convert_fusion.1.refs_0_), channel_id=1, source_target_pairs={{0,64},{64,0},{1,65},{65,1},{2,66},{66,2},{3,67},{67,3},{4,68},{68... | collective-permute-start | bytes 4128776 | tf_op jit(solution)/shard_map/ppermute | solution.py:53
  41.7 13.8 %collective-permute-start.12 = (bf16[128,2048]{1,0:T(8,128)(2,1)S(1)}, bf16[128,2048]{1,0:T(8,128)(2,1)S(1)}, u32[]{:S(2)}, u32[]{:S(2)}) collective-permute-start(bf16[128,2048]{1,0:T(8,128)(2,1)S(1)} %collective-permute-done.3.refs_2_), channel_id=1, source_target_pairs={{0,1},{1,2},{2,3},{3,0},{4,5},{5,6},{6,7},{7,4},{8,9},{9,10},{10,1... | collective-permute-start | bytes 1572872 | tf_op jit(solution)/shard_map/ppermute | solution.py:44
  43.1 12.4 %collective-permute-start.13 = (bf16[128,2048]{1,0:T(8,128)(2,1)S(1)}, bf16[128,2048]{1,0:T(8,128)(2,1)S(1)}, u32[]{:S(2)}, u32[]{:S(2)}) collective-permute-start(bf16[128,2048]{1,0:T(8,128)(2,1)S(1)} %collective-permute-done.7.refs_2_), channel_id=1, source_target_pairs={{0,16},{16,32},{32,48},{48,0},{64,112},{80,64},{96,80},{112,96},{1... | collective-permute-start | bytes 1572872 | tf_op jit(solution)/shard_map/ppermute | solution.py:44
  45.5 10.0 %collective-permute-start.14 = (bf16[128,2048]{1,0:T(8,128)(2,1)S(1)}, bf16[128,2048]{1,0:T(8,128)(2,1)S(1)}, u32[]{:S(2)}, u32[]{:S(2)}) collective-permute-start(bf16[128,2048]{1,0:T(8,128)(2,1)S(1)} %collective-permute-done.11.refs_2_), channel_id=1, source_target_pairs={{0,4},{1,5},{2,6},{3,7},{4,8},{5,9},{6,10},{7,11},{8,12},{9,13},{1... | collective-permute-start | bytes 1572872 | tf_op jit(solution)/shard_map/ppermute | solution.py:44
  55.2 13.9 %collective-permute-start.17 = (bf16[192,3584]{1,0:T(8,128)(2,1)S(1)}, bf16[192,3584]{1,0:T(8,128)(2,1)S(1)}, u32[]{:S(2)}, u32[]{:S(2)}) collective-permute-start(bf16[192,3584]{1,0:T(8,128)(2,1)S(1)} %convolution_convert_fusion.refs_2_), channel_id=1, source_target_pairs={{0,64},{64,0},{1,65},{65,1},{2,66},{66,2},{3,67},{67,3},{4,68},{68... | collective-permute-start | bytes 4128776 | tf_op jit(solution)/shard_map/ppermute | solution.py:53
  55.5 10.2 %collective-permute-start.19 = (bf16[128,2048]{1,0:T(8,128)(2,1)S(1)}, bf16[128,2048]{1,0:T(8,128)(2,1)S(1)}, u32[]{:S(2)}, u32[]{:S(2)}) collective-permute-start(bf16[128,2048]{1,0:T(8,128)(2,1)S(1)} %collective-permute-done.14.refs_3_), channel_id=1, source_target_pairs={{0,4},{1,5},{2,6},{3,7},{4,8},{5,9},{6,10},{7,11},{8,12},{9,13},{1... | collective-permute-start | bytes 1572872 | tf_op jit(solution)/shard_map/ppermute | solution.py:44
  57.3 8.4 %collective-permute-start.18 = (bf16[128,2048]{1,0:T(8,128)(2,1)S(1)}, bf16[128,2048]{1,0:T(8,128)(2,1)S(1)}, u32[]{:S(2)}, u32[]{:S(2)}) collective-permute-start(bf16[128,2048]{1,0:T(8,128)(2,1)S(1)} %collective-permute-done.13.refs_3_), channel_id=1, source_target_pairs={{0,16},{16,32},{32,48},{48,0},{64,112},{80,64},{96,80},{112,96},{1... | collective-permute-start | bytes 1572872 | tf_op jit(solution)/shard_map/ppermute | solution.py:44
  57.5 11.6 %collective-permute-start.15 = (bf16[128,2048]{1,0:T(8,128)(2,1)S(1)}, bf16[128,2048]{1,0:T(8,128)(2,1)S(1)}, u32[]{:S(2)}, u32[]{:S(2)}) collective-permute-start(bf16[128,2048]{1,0:T(8,128)(2,1)S(1)} %collective-permute-done.12.refs_3_), channel_id=1, source_target_pairs={{0,1},{1,2},{2,3},{3,0},{4,5},{5,6},{6,7},{7,4},{8,9},{9,10},{10,1... | collective-permute-start | bytes 1572872 | tf_op jit(solution)/shard_map/ppermute | solution.py:44
  65.9 28.2 %collective-permute-start.23 = (bf16[512,2048]{1,0:T(8,128)(2,1)S(1)}, bf16[512,2048]{1,0:T(8,128)(2,1)S(1)}, u32[]{:S(2)}, u32[]{:S(2)}) collective-permute-start(bf16[512,2048]{1,0:T(8,128)(2,1)S(1)} %shard_map.99.refs_2_.refs_5_.refs_4_), channel_id=1, source_target_pairs={{0,16},{16,32},{32,48},{48,0},{64,112},{80,64},{96,80},{112,96},{1... | collective-permute-start | bytes 6291464 | tf_op jit(solution)/shard_map/ppermute | solution.py:44
  67.4 28.7 %collective-permute-start.22 = (bf16[512,2048]{1,0:T(8,128)(2,1)S(1)}, bf16[512,2048]{1,0:T(8,128)(2,1)}, u32[]{:S(2)}, u32[]{:S(2)}) collective-permute-start(bf16[512,2048]{1,0:T(8,128)(2,1)S(1)} %shard_map.98.refs_1_.refs_4_.refs_3_), channel_id=1, source_target_pairs={{0,1},{1,2},{2,3},{3,0},{4,5},{5,6},{6,7},{7,4},{8,9},{9,10},{10,1... | collective-permute-start | bytes 6291464 | tf_op jit(solution)/shard_map/ppermute | solution.py:44
  70.2 28.8 %collective-permute-start.21 = (bf16[512,2048]{1,0:T(8,128)(2,1)S(1)}, bf16[512,2048]{1,0:T(8,128)(2,1)}, u32[]{:S(2)}, u32[]{:S(2)}) collective-permute-start(bf16[512,2048]{1,0:T(8,128)(2,1)S(1)} %shard_map.97.refs_0_.refs_3_.refs_2_), channel_id=1, source_target_pairs={{0,4},{1,5},{2,6},{3,7},{4,8},{5,9},{6,10},{7,11},{8,12},{9,13},{1... | collective-permute-start | bytes 6291464 | tf_op jit(solution)/shard_map/ppermute | solution.py:44
  70.5 14.6 %collective-permute-start.20 = (bf16[192,3584]{1,0:T(8,128)(2,1)}, bf16[192,3584]{1,0:T(8,128)(2,1)}, u32[]{:S(2)}, u32[]{:S(2)}) collective-permute-start(bf16[192,3584]{1,0:T(8,128)(2,1)} %shard_map.96.refs_4_), channel_id=1, source_target_pairs={{0,64},{64,0},{1,65},{65,1},{2,66},{66,2},{3,67},{67,3},{4,68},{68... | collective-permute-start | bytes 4128776 | tf_op jit(solution)/shard_map/ppermute | solution.py:53
  84.5 8.5 %collective-permute-start.24 = (bf16[3,256,768]{2,1,0:T(8,128)(2,1)S(1)}, bf16[3,256,768]{2,1,0:T(8,128)(2,1)S(1)}, u32[]{:S(2)}, u32[]{:S(2)}) collective-permute-start(bf16[3,256,768]{2,1,0:T(8,128)(2,1)S(1)} %shard_map.101.mine_ref.mine_grad_ref), channel_id=1, source_target_pairs={{0,64},{64,0},{1,65},{65,1},{2,66},{66,2},{3,67},{67,3},{4,68},{68... | collective-permute-start | bytes 3538952 | tf_op jit(solution)/shard_map/ppermute | solution.py:53
  94.0 32.1 %collective-permute-start.30 = (bf16[512,2048]{1,0:T(8,128)(2,1)S(1)}, bf16[512,2048]{1,0:T(8,128)(2,1)}, u32[]{:S(2)}, u32[]{:S(2)}) collective-permute-start(bf16[512,2048]{1,0:T(8,128)(2,1)S(1)} %collective-permute-done.23.refs_2_.refs_5_.refs_4_), channel_id=1, source_target_pairs={{0,16},{16,32},{32,48},{48,0},{64,112},{80,64},{96,80},{112,96},{1... | collective-permute-start | bytes 6291464 | tf_op jit(solution)/shard_map/ppermute | solution.py:44
  96.0 30.2 %collective-permute-start.28 = (bf16[512,2048]{1,0:T(8,128)(2,1)}, bf16[512,2048]{1,0:T(8,128)(2,1)}, u32[]{:S(2)}, u32[]{:S(2)}) collective-permute-start(bf16[512,2048]{1,0:T(8,128)(2,1)} %collective-permute-done.22.refs_1_.refs_4_.refs_3_), channel_id=1, source_target_pairs={{0,1},{1,2},{2,3},{3,0},{4,5},{5,6},{6,7},{7,4},{8,9},{9,10},{10,1... | collective-permute-start | bytes 6291464 | tf_op jit(solution)/shard_map/ppermute | solution.py:44
  99.0 28.5 %collective-permute-start.25 = (bf16[512,2048]{1,0:T(8,128)(2,1)}, bf16[512,2048]{1,0:T(8,128)(2,1)}, u32[]{:S(2)}, u32[]{:S(2)}) collective-permute-start(bf16[512,2048]{1,0:T(8,128)(2,1)} %collective-permute-done.21.refs_0_.refs_3_.refs_2_), channel_id=1, source_target_pairs={{0,4},{1,5},{2,6},{3,7},{4,8},{5,9},{6,10},{7,11},{8,12},{9,13},{1... | collective-permute-start | bytes 6291464 | tf_op jit(solution)/shard_map/ppermute | solution.py:44
  126.2 25.5 %collective-permute-start.31 = (bf16[512,2048]{1,0:T(8,128)(2,1)}, bf16[512,2048]{1,0:T(8,128)(2,1)S(1)}, u32[]{:S(2)}, u32[]{:S(2)}) collective-permute-start(bf16[512,2048]{1,0:T(8,128)(2,1)} %collective-permute-done.30.refs_2_.refs_5_.refs_7_), channel_id=1, source_target_pairs={{0,16},{16,32},{32,48},{48,0},{64,112},{80,64},{96,80},{112,96},{1... | collective-permute-start | bytes 6291464 | tf_op jit(solution)/shard_map/ppermute | solution.py:44
  126.3 25.5 %collective-permute-start.29 = (bf16[512,2048]{1,0:T(8,128)(2,1)}, bf16[512,2048]{1,0:T(8,128)(2,1)S(1)}, u32[]{:S(2)}, u32[]{:S(2)}) collective-permute-start(bf16[512,2048]{1,0:T(8,128)(2,1)} %collective-permute-done.28.refs_1_.refs_4_.refs_6_), channel_id=1, source_target_pairs={{0,1},{1,2},{2,3},{3,0},{4,5},{5,6},{6,7},{7,4},{8,9},{9,10},{10,1... | collective-permute-start | bytes 6291464 | tf_op jit(solution)/shard_map/ppermute | solution.py:44
  127.5 25.7 %collective-permute-start.27 = (bf16[512,2048]{1,0:T(8,128)(2,1)}, bf16[512,2048]{1,0:T(8,128)(2,1)}, u32[]{:S(2)}, u32[]{:S(2)}) collective-permute-start(bf16[512,2048]{1,0:T(8,128)(2,1)} %collective-permute-done.25.refs_0_.refs_3_.refs_5_), channel_id=1, source_target_pairs={{0,4},{1,5},{2,6},{3,7},{4,8},{5,9},{6,10},{7,11},{8,12},{9,13},{1... | collective-permute-start | bytes 6291464 | tf_op jit(solution)/shard_map/ppermute | solution.py:44
  160.9 16.4 %collective-permute-start.37 = (bf16[3,256,256]{2,1,0:T(8,128)(2,1)S(1)}, bf16[3,256,256]{2,1,0:T(8,128)(2,1)}, u32[]{:S(2)}, u32[]{:S(2)}) collective-permute-start(bf16[3,256,256]{2,1,0:T(8,128)(2,1)S(1)} %shard_map.117.mine_grad_ref), channel_id=1, source_target_pairs={{0,64},{64,0},{1,65},{65,1},{2,66},{66,2},{3,67},{67,3},{4,68},{68... | collective-permute-start | bytes 1179656 | tf_op jit(solution)/shard_map/ppermute | solution.py:53
  167.2 20.4 %collective-permute-start.34 = (bf16[96,2048]{1,0:T(8,128)(2,1)}, bf16[96,2048]{1,0:T(8,128)(2,1)}, u32[]{:S(2)}, u32[]{:S(2)}) collective-permute-start(bf16[96,2048]{1,0:T(8,128)(2,1)} %get-tuple-element.123), channel_id=1, source_target_pairs={{0,48},{16,0},{32,16},{48,32},{1,49},{17,1},{33,17},{49,33},{2,50}... | collective-permute-start | bytes 1179656 | tf_op jit(solution)/shard_map/ppermute | solution.py:49
  170.1 17.4 %collective-permute-start.35 = (bf16[96,2048]{1,0:T(8,128)(2,1)}, bf16[96,2048]{1,0:T(8,128)(2,1)}, u32[]{:S(2)}, u32[]{:S(2)}) collective-permute-start(bf16[96,2048]{1,0:T(8,128)(2,1)} %get-tuple-element.124), channel_id=1, source_target_pairs={{0,32},{16,48},{32,0},{48,16},{1,33},{17,49},{33,1},{49,17},{2,34}... | collective-permute-start | bytes 1179656 | tf_op jit(solution)/shard_map/ppermute | solution.py:49
  170.1 20.7 %collective-permute-start.36 = (bf16[96,2048]{1,0:T(8,128)(2,1)}, bf16[96,2048]{1,0:T(8,128)(2,1)}, u32[]{:S(2)}, u32[]{:S(2)}) collective-permute-start(bf16[96,2048]{1,0:T(8,128)(2,1)} %get-tuple-element.125), channel_id=1, source_target_pairs={{0,16},{16,32},{32,48},{48,0},{1,17},{17,33},{33,49},{49,1},{2,18}... | collective-permute-start | bytes 1179656 | tf_op jit(solution)/shard_map/ppermute | solution.py:49
  170.8 22.3 %all-to-all-start = ((bf16[16,224,128]{2,1,0:T(8,128)(2,1)}), bf16[16,224,128]{2,1,0:T(8,128)(2,1)}, u32[]{:S(2)}, u32[]{:S(2)}) async-start(bf16[16,224,128]{2,1,0:T(8,128)(2,1)} %copy-done.30), calls=%async_computation | async-start | bytes 1835008 | tf_op jit(solution)/shard_map/all_to_all | solution.py:477
  (52 other events, 314.6 us)
